TPU v7x, 512 devices: a whole 4x8x8 slice. The times are simulated.
512 devices in a mesh: blk: 128 (over y, x, z_lo, core), pitch: 4 (over z_hi).
Axes of the slice: x: 4, y: 8, z: 8 (z_hi: 4, z_lo: 2; z = z_hi * 2 + z_lo), core: 2. Of those that a mesh axis runs over, the one named last changes fastest.
Arguments:
- flow_state: float32 [5, 32, 2048, 128], P(None, 'pitch', 'blk'), may hold values from -0.6 to 3.2, as said below
- prior_state: float32 [5, 32, 2048, 128], P(None, 'pitch', 'blk'), may hold values from -0.75 to 3.35, as said below
- fourier_store: float32 [2, 49, 10, 2048, 128], P(None, None, None, ('blk', 'pitch')), may hold values from -0.15 to 2.6, as said below
- sample_times: int32 [2, 2048, 128], P(None, ('blk', 'pitch')), may hold values from 0 to 95
- harmonics: int32 [2048, 128], P(('blk', 'pitch')), may hold values from 12 to 24
Outputs:
- new_state: float32 [5, 32, 2048, 128], P(None, 'pitch', 'blk')
- new_store: float32 [2, 49, 10, 2048, 128], P(None, None, None, ('blk', 'pitch'))
- new_ghosts: float32 [2, 10, 2048, 128], P(None, None, ('blk', 'pitch'))
Inputs may be any that keep to these rules, and one draw needn't show every extreme that they name: `flow_state`: density between 0.7 and 1.3, momenta between -0.6 and 0.6, total energy between 2.2 and 3.2. `prior_state`: each entry within 0.15 of flow_state's. `fourier_store`: the k-th cosine and sine coefficients are at most 0.08 / k in magnitude.
All inputs are finite; a program needn't handle non-finite values.
Results may differ from a plain program's by a relative error of at most 0.000068.
Values sent between devices are 32-bit elements; how exact they have to be, the bound alone decides.
A program may use at most 64 MiB of HBM per device.

v0:
```python
import math

import jax
import jax.numpy as jnp
from jax import lax
from jax.sharding import PartitionSpec as P

NT = 96


gamma_less = 0.4
diss_coeff = 0.03125
section_coefs = (1.0 / 3.0, 0.5, 1.0)
pseudo_step = 0.1
physical_step = 0.25
relax_rate = 0.125
lag_turns = 0.3


def padded_2(block, sides, width):
    for axis, dim in sides:
        count = lax.axis_size(axis)
        forward = [(i, i + 1) for i in range(count - 1)]
        backward = [(target, source) for source, target in forward]
        low = lax.ppermute(
            lax.slice_in_dim(block, block.shape[dim] - width, None, axis=dim), axis, forward
        )
        high = lax.ppermute(lax.slice_in_dim(block, 0, width, axis=dim), axis, backward)
        block = jnp.concatenate([low, block, high], axis=dim)
    return block


def fluxes(current, direction):
    density = current[0]
    velocity = current[direction] / density
    pressure = gamma_less * (
        current[4]
        - 0.5
        * (current[1] * current[1] + current[2] * current[2] + current[3] * current[3])
        / density
    )
    flux_parts = [
        current[direction],
        current[1] * velocity,
        current[2] * velocity,
        current[3] * velocity,
        (current[4] + pressure) * velocity,
    ]
    flux_parts[direction] = flux_parts[direction] + pressure
    return jnp.stack(flux_parts)


def face_sum(padded, direction):
    cells_n = padded.shape[direction] - 4
    faces_n = cells_n + 1
    cell_flux = fluxes(padded, direction)

    def window(values, offset, length):
        return lax.slice_in_dim(values, offset, offset + length, axis=direction)

    face_flux = 0.5 * (
        window(cell_flux, 1, faces_n) + window(cell_flux, 2, faces_n)
    ) - diss_coeff * (
        window(padded, 3, faces_n)
        - 3.0 * window(padded, 2, faces_n)
        + 3.0 * window(padded, 1, faces_n)
        - window(padded, 0, faces_n)
    )
    return window(face_flux, 1, cells_n) - window(face_flux, 0, cells_n)


def harmonic_tables(phases_at, harm_count):
    orders = jnp.arange(1, harm_count + 1).astype(jnp.float32).reshape((harm_count, 1, 1))
    angles = orders * phases_at[None]
    return (jnp.cos(angles), jnp.sin(angles))


def rebuild(coeffs, phases_at, active):
    harm_count = (coeffs.shape[0] - 1) // 2
    cosines, sines = harmonic_tables(phases_at, harm_count)
    orders = jnp.arange(1, harm_count + 1).reshape((harm_count, 1, 1))
    active_mask = (orders <= active[None]).astype(jnp.float32)
    harm_terms = (
        coeffs[1 : harm_count + 1] * (active_mask * cosines)[:, None]
        + coeffs[harm_count + 1 :] * (active_mask * sines)[:, None]
    )
    return coeffs[0] + jnp.sum(harm_terms, axis=0)


def refresh(coeffs, samples, phases_at):
    harm_count = (coeffs.shape[0] - 1) // 2
    cosines, sines = harmonic_tables(phases_at, harm_count)
    mean_part = (1.0 - relax_rate) * coeffs[0] + relax_rate * samples
    cos_part = (1.0 - relax_rate) * coeffs[1 : harm_count + 1] + 2.0 * relax_rate * samples[
        None
    ] * cosines[:, None]
    sin_part = (1.0 - relax_rate) * coeffs[harm_count + 1 :] + 2.0 * relax_rate * samples[
        None
    ] * sines[:, None]
    return jnp.concatenate([mean_part[None], cos_part, sin_part], axis=0)


def shards(flow_state, prior_state, fourier_store, sample_times, harmonics):
    pitch_at = lax.axis_index("pitch")
    pitch_end = lax.axis_size("pitch") - 1
    blk_at = lax.axis_index("blk")
    blk_end = lax.axis_size("blk") - 1
    block_rows = flow_state.shape[2]
    radial_cells = flow_state.shape[3]
    period = 2.0 * math.pi / NT
    phase_lag = 2.0 * math.pi * lag_turns
    phases = sample_times.astype(jnp.float32) * period
    low_share = rebuild(fourier_store[0], phases[0] - phase_lag, harmonics)
    high_share = rebuild(fourier_store[1], phases[1] + phase_lag, harmonics)
    low_whole, high_whole = (
        lax.all_gather(low_share, "pitch", axis=1, tiled=True),
        lax.all_gather(high_share, "pitch", axis=1, tiled=True),
    )
    ghost_shape = (5, 2, block_rows, radial_cells)
    low_ghost = low_whole.reshape(ghost_shape)
    high_ghost = high_whole.reshape(ghost_shape)
    current = flow_state
    for section_coef in section_coefs:
        padded = padded_2(current, (("blk", 2), ("pitch", 1)), 2)
        pitch_pad = padded[:, :, 2:-2, :]
        axial_pad = padded[:, 2:-2, :, :]
        pitch_pad = jnp.concatenate(
            [
                jnp.where(pitch_at == 0, low_ghost, pitch_pad[:, :2]),
                current,
                jnp.where(pitch_at == pitch_end, high_ghost, pitch_pad[:, -2:]),
            ],
            axis=1,
        )
        lower_edge = jnp.broadcast_to(current[:, :, :1], axial_pad[:, :, :2].shape)
        upper_edge = jnp.broadcast_to(current[:, :, -1:], axial_pad[:, :, :2].shape)
        axial_pad = jnp.concatenate(
            [
                jnp.where(blk_at == 0, lower_edge, axial_pad[:, :, :2]),
                current,
                jnp.where(blk_at == blk_end, upper_edge, axial_pad[:, :, -2:]),
            ],
            axis=2,
        )
        radial_pad = jnp.pad(current, ((0, 0), (0, 0), (0, 0), (2, 2)), mode="edge")
        summed = face_sum(pitch_pad, 1) + face_sum(axial_pad, 2) + face_sum(radial_pad, 3)
        summed = summed + (3.0 * current - 4.0 * flow_state + prior_state) * (0.5 / physical_step)
        current = flow_state - section_coef * pseudo_step * summed
    face_shape = (10, block_rows, radial_cells)
    upper_face = current[:, -2:].reshape(face_shape)
    lower_face = current[:, :2].reshape(face_shape)
    nothing = jnp.zeros_like(lower_face)
    upper_mine, lower_mine = (
        lax.psum_scatter(
            jnp.where(pitch_at == pitch_end, upper_face, nothing),
            "pitch",
            scatter_dimension=1,
            tiled=True,
        ),
        lax.psum_scatter(
            jnp.where(pitch_at == 0, lower_face, nothing), "pitch", scatter_dimension=1, tiled=True
        ),
    )
    next_phases = phases + period
    low_store = refresh(fourier_store[0], upper_mine, next_phases[0])
    high_store = refresh(fourier_store[1], lower_mine, next_phases[1])
    ghosts = jnp.stack(
        [
            rebuild(low_store, next_phases[0] - phase_lag, harmonics),
            rebuild(high_store, next_phases[1] + phase_lag, harmonics),
        ]
    )
    return (current, jnp.stack([low_store, high_store]), ghosts)


def solution(mesh):
    placed = (
        P(None, "pitch", "blk", None),
        P(None, "pitch", "blk", None),
        P(None, None, None, ("blk", "pitch"), None),
        P(None, ("blk", "pitch"), None),
        P(("blk", "pitch"), None),
    )
    return jax.shard_map(
        shards,
        mesh=mesh,
        in_specs=placed,
        out_specs=(
            P(None, "pitch", "blk", None),
            P(None, None, None, ("blk", "pitch"), None),
            P(None, None, ("blk", "pitch"), None),
        ),
        check_vma=False,
    )
```

profile of v0, /device:TPU:1, one launch (start us, length us, event | category | flops | bytes accessed | tf_op | source)
XLA Modules:
  0.0 192.0 jit_solution(2830352598039493379)
XLA Ops:
  7.2 1.8 fusion.120
  9.0 8.8 %collective-permute-start.1 = (f32[5,8,2,128]{3,2,1,0:T(2,128)}, f32[5,8,2,128]{3,2,1,0:T(2,128)S(1)}, u32[]{:S(2)}, u32[]{:S(2)}) collective-permute-start(f32[5,8,2,128]{3,2,1,0:T(2,128)} %get-tuple-element.91), channel_id=1, source_target_pairs={{4,0},{8,4},{12,8},{16,12},{20,16},{24,20},{28,24},{32,28},{36,32}... | collective-permute-start | bytes 122888 | tf_op jit(solution)/shard_map/ppermute | solution.py:28
  17.8 1.9 %collective-permute-start = (f32[5,8,2,128]{3,2,1,0:T(2,128)}, f32[5,8,2,128]{3,2,1,0:T(2,128)}, u32[]{:S(2)}, u32[]{:S(2)}) collective-permute-start(f32[5,8,2,128]{3,2,1,0:T(2,128)} %get-tuple-element.92), channel_id=1, source_target_pairs={{0,4},{4,8},{8,12},{12,16},{16,20},{20,24},{24,28},{28,32},{32,36}... | collective-permute-start | bytes 122888 | tf_op jit(solution)/shard_map/ppermute | solution.py:25
  19.7 1.6 fusion.119
  21.4 1.2 fusion.121
  22.6 0.7 broadcast_add_fusion
  23.3 2.9 %multiply_sine_fusion.3 = (f32[24,4,128]{2,1,0:T(4,128)S(1)}, f32[24,4,128]{2,1,0:T(4,128)S(1)}, f32[24,4,128]{2,1,0:T(4,128)S(1)}, f32[24,4,128]{2,1,0:T(4,128)...) fusion(f32[4,128]{1,0:T(4,128)S(1)} %get-tuple-element.134, ...), kind=kLoop, calls=%fused_computation.261 | loop fusion | flops 184320 | bytes 604352 | tf_op jit(solution)/shard_map/sin | solution.py:75
  26.3 0.4 fusion.49
  26.7 0.6 bitcast_add_fusion
  27.3 0.6 copy.51
  29.4 1.1 fusion.16
  30.5 12.4 %all_gather.6 = f32[10,16,128]{2,0,1:T(8,128)S(1)} all-gather(f32[10,4,128]{2,0,1:T(8,128)S(1)} %copy-done.4), channel_id=1, replica_groups=mesh['blk'=128,'pitch'=4] {'pitch'}, dimensions={1}, use_global_device_ids=true | all-gather | bytes 102400 | tf_op jit(solution)/shard_map/all_gather | solution.py:116
  42.9 0.7 copy.53
  43.7 10.9 %all_gather.7 = f32[10,16,128]{2,0,1:T(8,128)S(1)} all-gather(f32[10,4,128]{2,0,1:T(8,128)S(1)} %copy.53), channel_id=1, replica_groups=mesh['blk'=128,'pitch'=4] {'pitch'}, dimensions={1}, use_global_device_ids=true | all-gather | bytes 102400 | tf_op jit(solution)/shard_map/all_gather | solution.py:117
  54.6 0.8 broadcast_select_fusion.2
  55.4 0.8 broadcast_select_fusion.5
  56.2 0.9 fusion.25
  57.1 1.3 collective-permute-start.3
  58.4 4.9 %collective-permute-start.2 = (f32[5,2,20,128]{3,2,1,0:T(8,128)S(1)}, f32[5,2,20,128]{3,2,1,0:T(8,128)S(1)}, u32[]{:S(2)}, u32[]{:S(2)}) collective-permute-start(f32[5,2,20,128]{3,2,1,0:T(8,128)S(1)} %get-tuple-element.72), channel_id=1, source_target_pairs={{0,1},{1,2},{2,3},{4,5},{5,6},{6,7},{8,9},{9,10},{10,11},{12,13},{... | collective-permute-start | bytes 307208 | tf_op jit(solution)/shard_map/ppermute | solution.py:25
  63.5 0.4 fusion.43
  64.0 1.3 collective-permute-done.2
  65.6 0.7 copy-done.2
  66.5 0.4 slice_reduce_fusion.2
  66.9 8.6 %collective-permute-start.5 = (f32[5,8,2,128]{3,2,1,0:T(2,128)S(1)}, f32[5,8,2,128]{3,2,1,0:T(2,128)S(1)}, u32[]{:S(2)}, u32[]{:S(2)}) collective-permute-start(f32[5,8,2,128]{3,2,1,0:T(2,128)S(1)} %get-tuple-element.85), channel_id=1, source_target_pairs={{4,0},{8,4},{12,8},{16,12},{20,16},{24,20},{28,24},{32,28},{36,32}... | collective-permute-start | bytes 122888 | tf_op jit(solution)/shard_map/ppermute | solution.py:28
  75.6 3.7 %collective-permute-start.4 = (f32[5,8,2,128]{3,2,1,0:T(2,128)S(1)}, f32[5,8,2,128]{3,2,1,0:T(2,128)S(1)}, u32[]{:S(2)}, u32[]{:S(2)}) collective-permute-start(f32[5,8,2,128]{3,2,1,0:T(2,128)S(1)} %get-tuple-element.86), channel_id=1, source_target_pairs={{0,4},{4,8},{8,12},{12,16},{16,20},{20,24},{24,28},{28,32},{32,36}... | collective-permute-start | bytes 122888 | tf_op jit(solution)/shard_map/ppermute | solution.py:25
  79.6 0.3 pad_maximum_fusion.8
  80.1 1.1 fusion.9
  81.5 1.3 collective-permute-start.7
  82.8 5.9 %collective-permute-start.6 = (f32[5,2,20,128]{3,2,1,0:T(8,128)S(1)}, f32[5,2,20,128]{3,2,1,0:T(8,128)S(1)}, u32[]{:S(2)}, u32[]{:S(2)}) collective-permute-start(f32[5,2,20,128]{3,2,1,0:T(8,128)S(1)} %get-tuple-element.70), channel_id=1, source_target_pairs={{0,1},{1,2},{2,3},{4,5},{5,6},{6,7},{8,9},{9,10},{10,11},{12,13},{... | collective-permute-start | bytes 307208 | tf_op jit(solution)/shard_map/ppermute | solution.py:25
  88.8 0.4 fusion.36
  89.2 3.1 %collective-permute-done.7 = f32[5,2,20,128]{3,2,1,0:T(8,128)S(1)} collective-permute-done((f32[5,2,20,128]{3,2,1,0:T(8,128)S(1)}, f32[5,2,20,128]{3,2,1,0:T(8,128)S(1)}, u32[]{:S(2)}, u32[]{:S(2)}) %collective-permute-start.7) | collective-permute-done | bytes 102432 | tf_op jit(solution)/shard_map/ppermute | solution.py:28
  92.9 0.4 slice_reduce_fusion
  93.3 2.0 %collective-permute-start.9 = (f32[5,8,2,128]{3,2,1,0:T(2,128)S(1)}, f32[5,8,2,128]{3,2,1,0:T(2,128)S(1)}, u32[]{:S(2)}, u32[]{:S(2)}) collective-permute-start(f32[5,8,2,128]{3,2,1,0:T(2,128)S(1)} %get-tuple-element.79), channel_id=1, source_target_pairs={{4,0},{8,4},{12,8},{16,12},{20,16},{24,20},{28,24},{32,28},{36,32}... | collective-permute-start | bytes 122888 | tf_op jit(solution)/shard_map/ppermute | solution.py:28
  95.3 5.0 %collective-permute-start.8 = (f32[5,8,2,128]{3,2,1,0:T(2,128)S(1)}, f32[5,8,2,128]{3,2,1,0:T(2,128)S(1)}, u32[]{:S(2)}, u32[]{:S(2)}) collective-permute-start(f32[5,8,2,128]{3,2,1,0:T(2,128)S(1)} %get-tuple-element.80), channel_id=1, source_target_pairs={{0,4},{4,8},{8,12},{12,16},{16,20},{20,24},{24,28},{28,32},{32,36}... | collective-permute-start | bytes 122888 | tf_op jit(solution)/shard_map/ppermute | solution.py:25
  101.1 1.1 fusion.2
  102.5 1.3 collective-permute-start.11
  103.8 7.2 %collective-permute-start.10 = (f32[5,2,20,128]{3,2,1,0:T(8,128)S(1)}, f32[5,2,20,128]{3,2,1,0:T(8,128)S(1)}, u32[]{:S(2)}, u32[]{:S(2)}) collective-permute-start(f32[5,2,20,128]{3,2,1,0:T(8,128)S(1)} %get-tuple-element.68), channel_id=1, source_target_pairs={{0,1},{1,2},{2,3},{4,5},{5,6},{6,7},{8,9},{9,10},{10,11},{12,13},{... | collective-permute-start | bytes 307208 | tf_op jit(solution)/shard_map/ppermute | solution.py:25
  111.2 0.4 fusion.29
  111.5 2.5 %collective-permute-done.11 = f32[5,2,20,128]{3,2,1,0:T(8,128)S(1)} collective-permute-done((f32[5,2,20,128]{3,2,1,0:T(8,128)S(1)}, f32[5,2,20,128]{3,2,1,0:T(8,128)S(1)}, u32[]{:S(2)}, u32[]{:S(2)}) %collective-permute-start.11) | collective-permute-done | bytes 102432 | tf_op jit(solution)/shard_map/ppermute | solution.py:28
  114.7 0.7 slice_select_fusion.1
  115.5 1.3 dynamic-slice
  117.4 61.6 %all-reduce.5.cloned.1.call-done = (f32[10,16,128]{2,1,0:T(8,128)}, f32[10,16,128]{2,1,0:T(8,128)}) async-done(((f32[10,16,128]{2,1,0:T(8,128)}, f32[10,16,128]{2,1,0:T(8,128)}), (f32[10,16,128]{2,1,0:T(8,128)}, f32[10,16,128]{2,1,0:T(8,128)})) %all-reduce.5.cloned.1.call-update) | async-done | bytes 163856
  178.9 0.8 dynamic-slice_multiply_fusion
  179.7 0.8 dynamic-slice_multiply_fusion.1
  180.5 0.9 add_reduce_fusion.1
  181.5 0.8 add_bitcast_fusion.1
  182.3 0.6 pad_maximum_fusion.31
  183.4 1.8 pad_maximum_fusion
  (109 shorter events, 5.7 us)
Async XLA Ops:
  7.2 19.1 %copy-start.1 = (f32[2,49,10,4,128]{4,3,2,1,0:T(4,128)S(1)}, f32[2,49,10,4,128]{4,3,2,1,0:T(4,128)}, u32[]{:S(2)}) copy-start(f32[2,49,10,4,128]{4,3,2,1,0:T(4,128)} %param.7) | copy-start | bytes 6021124
  7.2 171.8 %all-reduce.5.cloned.1.call-start = ((), (), s32[]{:S(2)}) async-start(), calls=%async_computation | async-start | bytes 327680
  9.0 45.6 %collective-permute-start.1 = (f32[5,8,2,128]{3,2,1,0:T(2,128)}, f32[5,8,2,128]{3,2,1,0:T(2,128)S(1)}, u32[]{:S(2)}, u32[]{:S(2)}) collective-permute-start(f32[5,8,2,128]{3,2,1,0:T(2,128)} %get-tuple-element.91), channel_id=1, source_target_pairs={{4,0},{8,4},{12,8},{16,12},{20,16},{24,20},{28,24},{32,28},{36,32}... | collective-permute-start | bytes 122888 | tf_op jit(solution)/shard_map/ppermute | solution.py:28
  17.8 37.6 %collective-permute-start = (f32[5,8,2,128]{3,2,1,0:T(2,128)}, f32[5,8,2,128]{3,2,1,0:T(2,128)}, u32[]{:S(2)}, u32[]{:S(2)}) collective-permute-start(f32[5,8,2,128]{3,2,1,0:T(2,128)} %get-tuple-element.92), channel_id=1, source_target_pairs={{0,4},{4,8},{8,12},{12,16},{16,20},{20,24},{24,28},{28,32},{32,36}... | collective-permute-start | bytes 122888 | tf_op jit(solution)/shard_map/ppermute | solution.py:25
  26.2 2.6 %copy-start = (f32[5,8,16,128]{3,2,1,0:T(8,128)S(1)}, f32[5,8,16,128]{3,2,1,0:T(8,128)}, u32[]{:S(2)}) copy-start(f32[5,8,16,128]{3,2,1,0:T(8,128)} %param.5) | copy-start | bytes 983044
  29.2 1.2 copy-start.4
  57.1 6.8 %collective-permute-start.3 = (f32[5,2,20,128]{3,2,1,0:T(8,128)S(1)}, f32[5,2,20,128]{3,2,1,0:T(8,128)S(1)}, u32[]{:S(2)}, u32[]{:S(2)}) collective-permute-start(f32[5,2,20,128]{3,2,1,0:T(8,128)S(1)} %get-tuple-element.71), channel_id=1, source_target_pairs={{1,0},{2,1},{3,2},{5,4},{6,5},{7,6},{9,8},{10,9},{11,10},{13,12},{... | collective-permute-start | bytes 307208 | tf_op jit(solution)/shard_map/ppermute | solution.py:28
  58.4 6.8 %collective-permute-start.2 = (f32[5,2,20,128]{3,2,1,0:T(8,128)S(1)}, f32[5,2,20,128]{3,2,1,0:T(8,128)S(1)}, u32[]{:S(2)}, u32[]{:S(2)}) collective-permute-start(f32[5,2,20,128]{3,2,1,0:T(8,128)S(1)} %get-tuple-element.72), channel_id=1, source_target_pairs={{0,1},{1,2},{2,3},{4,5},{5,6},{6,7},{8,9},{9,10},{10,11},{12,13},{... | collective-permute-start | bytes 307208 | tf_op jit(solution)/shard_map/ppermute | solution.py:25
  65.3 1.0 copy-start.2
  66.9 14.3 %collective-permute-start.5 = (f32[5,8,2,128]{3,2,1,0:T(2,128)S(1)}, f32[5,8,2,128]{3,2,1,0:T(2,128)S(1)}, u32[]{:S(2)}, u32[]{:S(2)}) collective-permute-start(f32[5,8,2,128]{3,2,1,0:T(2,128)S(1)} %get-tuple-element.85), channel_id=1, source_target_pairs={{4,0},{8,4},{12,8},{16,12},{20,16},{24,20},{28,24},{32,28},{36,32}... | collective-permute-start | bytes 122888 | tf_op jit(solution)/shard_map/ppermute | solution.py:28
  75.6 5.7 %collective-permute-start.4 = (f32[5,8,2,128]{3,2,1,0:T(2,128)S(1)}, f32[5,8,2,128]{3,2,1,0:T(2,128)S(1)}, u32[]{:S(2)}, u32[]{:S(2)}) collective-permute-start(f32[5,8,2,128]{3,2,1,0:T(2,128)S(1)} %get-tuple-element.86), channel_id=1, source_target_pairs={{0,4},{4,8},{8,12},{12,16},{16,20},{20,24},{24,28},{28,32},{32,36}... | collective-permute-start | bytes 122888 | tf_op jit(solution)/shard_map/ppermute | solution.py:25
  81.5 10.8 %collective-permute-start.7 = (f32[5,2,20,128]{3,2,1,0:T(8,128)S(1)}, f32[5,2,20,128]{3,2,1,0:T(8,128)S(1)}, u32[]{:S(2)}, u32[]{:S(2)}) collective-permute-start(f32[5,2,20,128]{3,2,1,0:T(8,128)S(1)} %get-tuple-element.69), channel_id=1, source_target_pairs={{1,0},{2,1},{3,2},{5,4},{6,5},{7,6},{9,8},{10,9},{11,10},{13,12},{... | collective-permute-start | bytes 307208 | tf_op jit(solution)/shard_map/ppermute | solution.py:28
  82.8 9.5 %collective-permute-start.6 = (f32[5,2,20,128]{3,2,1,0:T(8,128)S(1)}, f32[5,2,20,128]{3,2,1,0:T(8,128)S(1)}, u32[]{:S(2)}, u32[]{:S(2)}) collective-permute-start(f32[5,2,20,128]{3,2,1,0:T(8,128)S(1)} %get-tuple-element.70), channel_id=1, source_target_pairs={{0,1},{1,2},{2,3},{4,5},{5,6},{6,7},{8,9},{9,10},{10,11},{12,13},{... | collective-permute-start | bytes 307208 | tf_op jit(solution)/shard_map/ppermute | solution.py:25
  93.3 9.0 %collective-permute-start.9 = (f32[5,8,2,128]{3,2,1,0:T(2,128)S(1)}, f32[5,8,2,128]{3,2,1,0:T(2,128)S(1)}, u32[]{:S(2)}, u32[]{:S(2)}) collective-permute-start(f32[5,8,2,128]{3,2,1,0:T(2,128)S(1)} %get-tuple-element.79), channel_id=1, source_target_pairs={{4,0},{8,4},{12,8},{16,12},{20,16},{24,20},{28,24},{32,28},{36,32}... | collective-permute-start | bytes 122888 | tf_op jit(solution)/shard_map/ppermute | solution.py:28
  95.3 7.0 %collective-permute-start.8 = (f32[5,8,2,128]{3,2,1,0:T(2,128)S(1)}, f32[5,8,2,128]{3,2,1,0:T(2,128)S(1)}, u32[]{:S(2)}, u32[]{:S(2)}) collective-permute-start(f32[5,8,2,128]{3,2,1,0:T(2,128)S(1)} %get-tuple-element.80), channel_id=1, source_target_pairs={{0,4},{4,8},{8,12},{12,16},{16,20},{20,24},{24,28},{28,32},{32,36}... | collective-permute-start | bytes 122888 | tf_op jit(solution)/shard_map/ppermute | solution.py:25
  102.5 11.5 %collective-permute-start.11 = (f32[5,2,20,128]{3,2,1,0:T(8,128)S(1)}, f32[5,2,20,128]{3,2,1,0:T(8,128)S(1)}, u32[]{:S(2)}, u32[]{:S(2)}) collective-permute-start(f32[5,2,20,128]{3,2,1,0:T(8,128)S(1)} %get-tuple-element.67), channel_id=1, source_target_pairs={{1,0},{2,1},{3,2},{5,4},{6,5},{7,6},{9,8},{10,9},{11,10},{13,12},{... | collective-permute-start | bytes 307208 | tf_op jit(solution)/shard_map/ppermute | solution.py:28
  103.8 10.3 %collective-permute-start.10 = (f32[5,2,20,128]{3,2,1,0:T(8,128)S(1)}, f32[5,2,20,128]{3,2,1,0:T(8,128)S(1)}, u32[]{:S(2)}, u32[]{:S(2)}) collective-permute-start(f32[5,2,20,128]{3,2,1,0:T(8,128)S(1)} %get-tuple-element.68), channel_id=1, source_target_pairs={{0,1},{1,2},{2,3},{4,5},{5,6},{6,7},{8,9},{9,10},{10,11},{12,13},{... | collective-permute-start | bytes 307208 | tf_op jit(solution)/shard_map/ppermute | solution.py:25
  114.7 66.8 %copy-start.3 = (f32[5,8,16,128]{3,2,1,0:T(8,128)}, f32[5,8,16,128]{3,2,1,0:T(8,128)S(1)}, u32[]{:S(2)}) copy-start(f32[5,8,16,128]{3,2,1,0:T(8,128)S(1)} %fusion.89) | copy-start | bytes 983044
Sparse Core Ops, SparseCore 0:
  115.6 63.3 all-reduce.4
where the time goes:
time: 194 us; the launch traced here: 192 us
  waiting for transfers between devices  68.5 us (35%)
  starting transfers between devices  51.9 us (27%)
  blocking collectives  23.3 us (12%)
  other arithmetic  22.2 us (11%)
  between operations  15.5 us (8%)
  local copies, waits for them, and re-layouts  10.5 us (5%)
    unnamed x2, waiting for transfers between devices  61.6 us
    ppermute x6, starting transfers between devices, padded_2(): lax.ppermute(lax.slice_in_dim(block, block.shape[dim] - width, None, axis...  28.6 us
    ppermute x6, starting transfers between devices, padded_2(): lax.ppermute(lax.slice_in_dim(block, 0, width, axis=dim), axis, backward)  23.3 us
    all_gather x1, blocking collectives, shards(): lax.all_gather(low_share, 'pitch', axis=1, tiled=True)  12.4 us
    all_gather x1, blocking collectives, shards(): lax.all_gather(high_share, 'pitch', axis=1, tiled=True)  10.9 us
    ppermute x6, waiting for transfers between devices, padded_2(): lax.ppermute(lax.slice_in_dim(block, 0, width, axis=dim), axis, backward)  5.65 us
    sub x9, other arithmetic, face_sum(): 0.5 * (window(cell_flux, 1, faces_n) + window(cell_flux, 2, faces_n))  4.7 us
  transfers between devices with their start and end apart: 13, of which 4 were waited for; matrix products, arithmetic and copies ran while one was open for 10% of the time, Pallas kernels for 0%

commit v1 on v0

v1 whole, which is shorter than its diff:
```python
import functools
import math

import jax
import jax.numpy as jnp
from jax import lax
from jax.experimental import pallas as pl
from jax.experimental.pallas import tpu as pltpu
from jax.sharding import PartitionSpec as P

MESH = pl.DeviceIdType.MESH
F32 = jnp.float32
NT = 96
HARM = 24
COEFS = 2 * HARM + 1
PERIOD = 2.0 * math.pi / NT
LAG = 2.0 * math.pi * 0.3
SECTIONS = (1.0 / 3.0, 0.5, 1.0)
CENTER = (8, 16)
EXTENDED = (4, 12, 20)


def twice(ref):
    rows = ref[...]
    return jnp.concatenate([rows, rows], axis=0)


def base_turn(times):
    quarter = (times - NT // 2).astype(F32) * (PERIOD / 4.0)
    sq = quarter * quarter
    s = quarter * (1.0 + sq * (-1.0 / 6 + sq * (1.0 / 120 + sq * (-1.0 / 5040 + sq * (1.0 / 362880)))))
    c = 1.0 + sq * (
        -0.5 + sq * (1.0 / 24 + sq * (-1.0 / 720 + sq * (1.0 / 40320 + sq * (-1.0 / 3628800))))
    )
    for _ in range(2):
        c, s = 1.0 - 2.0 * s * s, 2.0 * s * c
    return -c, -s


def turned(turn, angle):
    c, s = turn
    ca, sa = math.cos(angle), math.sin(angle)
    return c * ca - s * sa, s * ca + c * sa


def times_turn(a, b):
    return a[0] * b[0] - a[1] * b[1], a[1] * b[0] + a[0] * b[1]


def half_flux(cell, direction):
    rho, mp, ma, mr, energy = cell
    half_inv = 0.5 / rho
    kinetic = (mp * mp + ma * ma + mr * mr) * half_inv
    half_p = 0.2 * (energy - kinetic)
    moment = cell[direction]
    half_u = moment * half_inv
    parts = [
        0.5 * moment,
        mp * half_u,
        ma * half_u,
        mr * half_u,
        (energy + (half_p + half_p)) * half_u,
    ]
    parts[direction] = parts[direction] + half_p
    return parts


def section(s, cur, flow, prior, out, out_offsets, first, count, rows):
    step = 0.1 * SECTIONS[s]
    lane = lax.broadcasted_iota(jnp.int32, (8, 128), 1)
    at_low, at_high = lane == 0, lane == 127

    def after(x):
        return jnp.where(at_high, x, pltpu.roll(x, 127, 1))

    def before(x):
        return jnp.where(at_low, x, pltpu.roll(x, 1, 1))

    def layer(i, carry):
        at = first + i
        li = at + 2
        for r0 in rows:

            def load(dl, dr):
                return [cur[v, li + dl, r0 + dr : r0 + dr + 8, :] for v in range(5)]

            mid = load(0, 0)
            near = [load(1, 0), load(-1, 0), load(0, 1), load(0, -1)]
            far = [load(2, 0), load(-2, 0), load(0, 2), load(0, -2)]
            fluxes = [half_flux(near[k], 1 + k // 2) for k in range(4)]
            radial = half_flux(mid, 3)
            for v in range(5):
                total = (fluxes[0][v] - fluxes[1][v]) + (fluxes[2][v] - fluxes[3][v])
                n1 = (near[0][v] + near[1][v]) + (near[2][v] + near[3][v])
                n2 = (far[0][v] + far[1][v]) + (far[2][v] + far[3][v])
                x = mid[v]
                eighth = 0.125 * x
                up = (eighth + radial[v]) - 0.03125 * after(x)
                down = (eighth - radial[v]) - 0.03125 * before(x)
                total = total + (after(up) + before(down)) + (0.125 * n1 - 0.03125 * n2)
                base = (1.0 + 8.0 * step) * flow[v, li, r0 : r0 + 8, :] - (
                    2.0 * step
                ) * prior[v, at, r0 : r0 + 8, :]
                new = base - (6.0 - 0.5625) * step * x - step * total
                out[v, at + out_offsets[0], r0 + out_offsets[1] : r0 + out_offsets[1] + 8, :] = new
        return carry

    lax.fori_loop(0, count, layer, 0)


def sections_kernel(
    flow_hbm, prior_hbm, store_hbm, times_hbm, harm_hbm,
    state_out, samples_out,
    u0, u1, u2, prior, store, times, harm, share, ghosts,
    pack, land, faces, samples,
    local_sem, send_sem, recv_sem, ready_sem,
):
    p = lax.axis_index("pitch")
    b = lax.axis_index("blk")
    n_blk = lax.axis_size("blk")
    n_pitch = lax.axis_size("pitch")
    first_p, last_p = p == 0, p == n_pitch - 1
    is_end = jnp.logical_or(first_p, last_p)
    b_low, b_high = b > 0, b < n_blk - 1
    pitch_up = {"pitch": lax.rem(p + 1, n_pitch)}
    pitch_down = {"pitch": lax.rem(p + n_pitch - 1, n_pitch)}
    states = (u0, u1, u2)

    barrier = pltpu.get_barrier_semaphore()
    for where in (pitch_up, pitch_down):
        pl.semaphore_signal(barrier, inc=1, device_id=where, device_id_type=MESH)
    for where, cond in (({"blk": b - 1}, b_low), ({"blk": b + 1}, b_high)):

        @pl.when(cond)
        def _():
            pl.semaphore_signal(barrier, inc=1, device_id=where, device_id_type=MESH)

    loads = [
        pltpu.make_async_copy(flow_hbm, u0.at[:, 2:10, 8:24, :], local_sem.at[0]),
        pltpu.make_async_copy(store_hbm.at[0], store.at[0], local_sem.at[1]),
        pltpu.make_async_copy(store_hbm.at[1], store.at[1], local_sem.at[2]),
        pltpu.make_async_copy(prior_hbm, prior.at[:, :, 8:24, :], local_sem.at[3]),
        pltpu.make_async_copy(times_hbm, times, local_sem.at[4]),
        pltpu.make_async_copy(harm_hbm, harm, local_sem.at[5]),
    ]
    for k in (0, 4, 5, 1, 2, 3):
        loads[k].start()

    pl.semaphore_wait(barrier, 2 + b_low.astype(jnp.int32) + b_high.astype(jnp.int32))

    sent = []
    counter = [0]

    def remote(src, dst, where, send_if, recv_if):
        k = counter[0]
        counter[0] += 1
        copy = pltpu.make_async_remote_copy(
            src_ref=src,
            dst_ref=dst,
            send_sem=send_sem.at[k],
            recv_sem=recv_sem.at[k],
            device_id=where,
            device_id_type=MESH,
        )
        return copy, send_if, recv_if

    def send(*copies):
        for copy, send_if, _ in copies:
            sent.append((copy, send_if))

            @pl.when(send_if)
            def _():
                copy.start()

    def arrive(*copies):
        for copy, _, recv_if in copies:

            @pl.when(recv_if)
            def _():
                copy.wait_recv()

    not_first, not_last = p > 0, p < n_pitch - 1

    def pitch_pair(src, offset, target):
        return (
            remote(
                src.at[:, offset + 6 : offset + 8, 8 * (offset // 2) : 8 * (offset // 2) + 16, :],
                target.at[:, 0:2, 8:24, :], pitch_up, not_last, not_first,
            ),
            remote(
                src.at[:, offset : offset + 2, 8 * (offset // 2) : 8 * (offset // 2) + 16, :],
                target.at[:, 10:12, 8:24, :], pitch_down, not_first, not_last,
            ),
        )

    pitch = [pitch_pair(flow_hbm, 0, u0), pitch_pair(u1, 2, u1), pitch_pair(u2, 2, u2)]
    send(*pitch[0])

    g4 = jnp.where(first_p, 0, 4)
    up_ok, down_ok = jnp.logical_and(is_end, b_high), jnp.logical_and(is_end, b_low)
    wide = [
        remote(
            flow_hbm.at[:, pl.ds(g4, 4), 8:16, :], u0.at[:, pl.ds(2 + g4, 4), 0:8, :],
            {"blk": b + 1}, up_ok, down_ok,
        ),
        remote(
            flow_hbm.at[:, pl.ds(g4, 4), 0:8, :], u0.at[:, pl.ds(2 + g4, 4), 24:32, :],
            {"blk": b - 1}, down_ok, up_ok,
        ),
        remote(
            prior_hbm.at[:, pl.ds(g4, 4), 8:16, :], prior.at[:, pl.ds(g4, 4), 0:8, :],
            {"blk": b + 1}, up_ok, down_ok,
        ),
        remote(
            prior_hbm.at[:, pl.ds(g4, 4), 0:8, :], prior.at[:, pl.ds(g4, 4), 24:32, :],
            {"blk": b - 1}, down_ok, up_ok,
        ),
    ]

    for k, where in enumerate((pitch_up, pitch_down)):
        pl.semaphore_signal(ready_sem.at[k], inc=1, device_id=where, device_id_type=MESH)

    parts = ((2, 3, 4, 5), (0, 1, 6, 7))
    axial = [
        [
            (
                remote(pack.at[s, part, 0], land.at[s, part, 0], {"blk": b + 1}, b_high, b_low),
                remote(pack.at[s, part, 1], land.at[s, part, 1], {"blk": b - 1}, b_low, b_high),
            )
            for part in range(2)
        ]
        for s in range(3)
    ]

    def axial_send(s, part):
        for side, row in ((0, 22), (1, 8)):
            for v in range(5):
                for k, at in enumerate(parts[part]):
                    pack[s, part, side, v, 2 * k : 2 * k + 2, :] = states[s][
                        v, 2 + at, row : row + 2, :
                    ]
        send(*axial[s][part])

    def axial_take(s, part):
        for side, row, cond in ((0, 6, b_low), (1, 24, b_high)):

            @pl.when(cond)
            def _():
                axial[s][part][side][0].wait_recv()
                for v in range(5):
                    for k, at in enumerate(parts[part]):
                        states[s][v, 2 + at, row : row + 2, :] = land[
                            s, part, side, v, 2 * k : 2 * k + 2, :
                        ]

    def fill_edges(s, first, count):
        ref = states[s]
        for cond, row, source in ((b == 0, 6, 8), (b == n_blk - 1, 24, 23)):

            @pl.when(cond)
            def _():
                def layer(i, carry):
                    for v in range(5):
                        edge = ref[v, 2 + first + i, source : source + 1, :]
                        ref[v, 2 + first + i, row : row + 2, :] = jnp.broadcast_to(edge, (2, 128))
                    return carry

                lax.fori_loop(0, count, layer, 0)

    loads[0].wait()
    axial_send(0, 0)
    axial_send(0, 1)
    send(*wide)

    for k in (4, 5):
        loads[k].wait()
    count8 = twice(harm)
    for x in range(2):
        loads[1 + x].wait()
        turn = turned(base_turn(twice(times.at[x])), LAG if x else -LAG)

        def harmonic(k, carry):
            now, total = carry
            keep = k <= count8
            c, s = jnp.where(keep, now[0], 0.0), jnp.where(keep, now[1], 0.0)
            total = tuple(
                total[j]
                + (
                    store[x, k, 8 * j : 8 * j + 8, :] * c
                    + store[x, HARM + k, 8 * j : 8 * j + 8, :] * s
                )
                for j in range(5)
            )
            return times_turn(now, turn), total

        start = tuple(store[x, 0, 8 * j : 8 * j + 8, :] for j in range(5))
        _, total = lax.fori_loop(1, HARM + 1, harmonic, (turn, start))
        for j in range(5):
            share[x, 8 * j : 8 * j + 8, :] = total[j]

    for k in range(2):
        pl.semaphore_wait(ready_sem.at[k], 1)

    ghost_copies = []
    for j in range(4):
        for x, target in ((0, 0), (1, 3)):
            if j != target:
                ghost_copies.append(
                    (
                        j,
                        x,
                        remote(
                            share.at[x], ghosts.at[1 + j], {"pitch": target},
                            p == j, p == target,
                        ),
                    )
                )
    beside = []
    for x, target in ((0, 0), (1, 3)):
        beside.append(
            remote(
                share.at[x], ghosts.at[0], {"blk": b + 1, "pitch": target},
                jnp.logical_and(last_p, b_high), jnp.logical_and(p == target, b_low),
            )
        )
        beside.append(
            remote(
                share.at[x], ghosts.at[5], {"blk": b - 1, "pitch": target},
                jnp.logical_and(first_p, b_low), jnp.logical_and(p == target, b_high),
            )
        )
    ghost_copies = [c[2] for c in ghost_copies] + beside
    send(*ghost_copies)
    for x, cond, slot in ((0, first_p, 1), (1, last_p, 4)):

        @pl.when(cond)
        def _():
            ghosts[slot] = share[x]

    def inner(s):
        fill_edges(s, 0, 8)
        if s < 2:
            section(s, states[s], u0, prior, states[s + 1], (2, 0), 2, 4, CENTER)
        else:
            section(s, states[s], u0, prior, state_out, (0, -8), 2, 4, CENTER)

    def pair(s, first):
        if s < 2:
            section(s, states[s], u0, prior, states[s + 1], (2, 0), first, 2, CENTER)
        else:
            section(s, states[s], u0, prior, state_out, (0, -8), first, 2, CENTER)

    def outer(s):
        for side, cond, first in ((1, not_last, 6), (0, not_first, 0)):

            @pl.when(cond)
            def _():
                pitch[s][side][0].wait_recv()
                pair(s, first)
                if s < 2:
                    pitch[s + 1][1 - side][0].start()

        if s < 2:
            sent.extend((c[0], c[1]) for c in pitch[s + 1])

    loads[3].wait()
    arrive(*wide[:2])
    axial_take(0, 0)
    axial_take(0, 1)
    inner(0)
    axial_send(1, 0)
    outer(0)
    axial_send(1, 1)

    face_copies = []
    for x, source in ((0, 3), (1, 0)):
        for j in range(4):
            if j != source:
                face_copies.append(
                    remote(faces.at[j], samples.at[x], {"pitch": j}, p == source, p == j)
                )

    @pl.when(is_end)
    def _():
        arrive(*wide[2:])
        arrive(*ghost_copies)
        g2 = jnp.where(first_p, 0, 10)
        for k in range(6):

            @pl.when(jnp.logical_or(jnp.logical_and(k > 0, k < 5), b_low if k == 0 else b_high))
            def _():
                for v in range(5):
                    for layer in range(2):
                        at = (2 * v + layer) * 4
                        block = ghosts[k, at : at + 4, :]
                        for ref in states:
                            ref[v, g2 + layer, 4 + 4 * k : 8 + 4 * k, :] = block

        near = jnp.where(first_p, 0, 6)
        beyond = jnp.where(first_p, 2, 4)
        section(0, u0, u0, prior, u1, (2, 0), near, 2, EXTENDED)
        section(0, u0, u0, prior, u1, (2, 0), beyond, 2, EXTENDED)
        fill_edges(1, g4, 4)
        section(1, u1, u0, prior, u2, (2, 0), near, 2, EXTENDED)
        section(1, u1, u0, prior, u2, (2, 0), beyond, 2, CENTER)
        fill_edges(2, g4, 4)
        section(2, u2, u0, prior, state_out, (0, -8), near, 2, CENTER)
        for j in range(4):
            for v in range(5):
                for layer in range(2):
                    at = (2 * v + layer) * 4
                    faces[j, at : at + 4, :] = state_out[v, near + layer, 4 * j : 4 * j + 4, :]

    send(*face_copies)
    for x, cond, slot in ((1, first_p, 0), (0, last_p, 3)):

        @pl.when(cond)
        def _():
            samples[x] = faces[slot]

    for s in (1, 2):
        axial_take(s, 0)
        axial_take(s, 1)
        inner(s)
        if s == 1:
            axial_send(2, 0)
        outer(s)
        if s == 1:
            axial_send(2, 1)

    arrive(*face_copies)
    samples_out[...] = samples[...]
    for copy, cond in sent:

        @pl.when(cond)
        def _():
            copy.wait_send()


GROUPS = 4


def store_kernel(
    store_hbm, times_ref, harm_ref, samples, state, store_out, ghosts_out, state_out,
    store, fresh, in_sem, out_sem,
):
    per = HARM // GROUPS
    fetch, write = {}, {}
    for x in range(2):
        for g in range(GROUPS):
            for half in range(2):
                at = 1 + HARM * half + per * g
                rows, k = pl.ds(at, per), (x * GROUPS + g) * 2 + half
                fetch[x, g, half] = pltpu.make_async_copy(
                    store_hbm.at[x, rows], store.at[x, rows], in_sem.at[k]
                )
                write[x, g, half] = pltpu.make_async_copy(
                    fresh.at[x, rows], store_out.at[x, rows], out_sem.at[k]
                )
        fetch[x, 0, 2] = pltpu.make_async_copy(
            store_hbm.at[x, 0], store.at[x, 0], in_sem.at[4 * GROUPS + x]
        )
        write[x, 0, 2] = pltpu.make_async_copy(
            fresh.at[x, 0], store_out.at[x, 0], out_sem.at[4 * GROUPS + x]
        )
    for x in range(2):
        fetch[x, 0, 2].start()
        for g in range(GROUPS):
            for half in range(2):
                fetch[x, g, half].start()
    state_copy = pltpu.make_async_copy(state, state_out, out_sem.at[4 * GROUPS + 2])
    state_copy.start()
    count8 = twice(harm_ref)
    for x in range(2):
        turn = turned(base_turn(twice(times_ref.at[x])), PERIOD)
        lagged = turned(turn, LAG if x else -LAG)
        seen = tuple(samples[x, 8 * j : 8 * j + 8, :] for j in range(5))
        fetch[x, 0, 2].wait()
        total = tuple(
            0.875 * store[x, 0, 8 * j : 8 * j + 8, :] + 0.125 * seen[j] for j in range(5)
        )
        for j in range(5):
            fresh[x, 0, 8 * j : 8 * j + 8, :] = total[j]
        write[x, 0, 2].start()
        carry = (turn, lagged, total)

        def harmonic(k, carry):
            now, late, total = carry
            keep = k <= count8
            c, s = jnp.where(keep, late[0], 0.0), jnp.where(keep, late[1], 0.0)
            wc, ws = 0.25 * now[0], 0.25 * now[1]
            sums = []
            for j in range(5):
                rows = slice(8 * j, 8 * j + 8)
                new_c = 0.875 * store[x, k, rows, :] + wc * seen[j]
                new_s = 0.875 * store[x, HARM + k, rows, :] + ws * seen[j]
                fresh[x, k, rows, :] = new_c
                fresh[x, HARM + k, rows, :] = new_s
                sums.append(total[j] + (new_c * c + new_s * s))
            return times_turn(now, turn), times_turn(late, lagged), tuple(sums)

        for g in range(GROUPS):
            for half in range(2):
                fetch[x, g, half].wait()
            carry = lax.fori_loop(1 + per * g, 1 + per * (g + 1), harmonic, carry)
            for half in range(2):
                write[x, g, half].start()
        for j in range(5):
            ghosts_out[x, 8 * j : 8 * j + 8, :] = carry[2][j]
    for copy in write.values():
        copy.wait()
    state_copy.wait()


def shards(flow_state, prior_state, fourier_store, sample_times, harmonics):
    cells = flow_state.shape
    store_flat = fourier_store.reshape(2, COEFS, 40, 128)
    anywhere = pl.BlockSpec(memory_space=pl.ANY)
    vmem = pl.BlockSpec(memory_space=pltpu.VMEM)
    state, samples = pl.pallas_call(
        sections_kernel,
        out_shape=(
            jax.ShapeDtypeStruct(cells, F32),
            jax.ShapeDtypeStruct((2, 40, 128), F32),
        ),
        in_specs=[anywhere] * 5,
        out_specs=(vmem, vmem),
        scratch_shapes=[
            pltpu.VMEM((5, 12, 32, 128), F32),
            pltpu.VMEM((5, 12, 32, 128), F32),
            pltpu.VMEM((5, 12, 32, 128), F32),
            pltpu.VMEM((5, 8, 32, 128), F32),
            pltpu.VMEM((2, COEFS, 40, 128), F32),
            pltpu.VMEM((2, 4, 128), jnp.int32),
            pltpu.VMEM((4, 128), jnp.int32),
            pltpu.VMEM((2, 40, 128), F32),
            pltpu.VMEM((6, 40, 128), F32),
            pltpu.VMEM((3, 2, 2, 5, 8, 128), F32),
            pltpu.VMEM((3, 2, 2, 5, 8, 128), F32),
            pltpu.VMEM((4, 40, 128), F32),
            pltpu.VMEM((2, 40, 128), F32),
            pltpu.SemaphoreType.DMA((6,)),
            pltpu.SemaphoreType.DMA((48,)),
            pltpu.SemaphoreType.DMA((48,)),
            pltpu.SemaphoreType.REGULAR((2,)),
        ],
        compiler_params=pltpu.CompilerParams(
            collective_id=0, has_side_effects=True, vmem_limit_bytes=24 * 1024 * 1024
        ),
        name="sections",
    )(flow_state, prior_state, store_flat, sample_times, harmonics)
    new_store, ghosts, new_state = pl.pallas_call(
        store_kernel,
        out_shape=(
            jax.ShapeDtypeStruct(store_flat.shape, F32),
            jax.ShapeDtypeStruct((2, 40, 128), F32),
            jax.ShapeDtypeStruct(cells, F32),
        ),
        in_specs=[anywhere, vmem, vmem, vmem, vmem],
        out_specs=(anywhere, vmem, anywhere),
        scratch_shapes=[
            pltpu.VMEM((2, COEFS, 40, 128), F32),
            pltpu.VMEM((2, COEFS, 40, 128), F32),
            pltpu.SemaphoreType.DMA((4 * GROUPS + 2,)),
            pltpu.SemaphoreType.DMA((4 * GROUPS + 3,)),
        ],
        compiler_params=pltpu.CompilerParams(vmem_limit_bytes=24 * 1024 * 1024),
        name="store",
    )(store_flat, sample_times, harmonics, samples, state)
    return (
        new_state,
        new_store.reshape(fourier_store.shape),
        ghosts.reshape(2, 10, 4, 128),
    )


def solution(mesh):
    placed = (
        P(None, "pitch", "blk", None),
        P(None, "pitch", "blk", None),
        P(None, None, None, ("blk", "pitch"), None),
        P(None, ("blk", "pitch"), None),
        P(("blk", "pitch"), None),
    )
    return jax.shard_map(
        shards,
        mesh=mesh,
        in_specs=placed,
        out_specs=(
            P(None, "pitch", "blk", None),
            P(None, None, None, ("blk", "pitch"), None),
            P(None, None, ("blk", "pitch"), None),
        ),
        check_vma=False,
    )
```

time: 194 us -> 42.2 us (0.22)
  waiting for transfers between devices: 68.5 us -> 0 us
  starting transfers between devices: 51.9 us -> 0 us
  Pallas kernels: 0 us -> 36.4 us
  blocking collectives: 23.3 us -> 0 us
  other arithmetic: 22.2 us -> 0 us
  between operations: 15.5 us -> 0.66 us
  local copies, waits for them, and re-layouts: 10.5 us -> 4.87 us
    unnamed x2 -> x0, waiting for transfers between devices: 61.6 us -> none
    ppermute x12 -> x0, starting transfers between devices: 51.9 us -> none  [the longest x6 28.6 us: padded_2(): lax.ppermute(lax.slice_in_dim(block, block.shape[dim] - width, None, axis...]
    pallas_call x0 -> x2, Pallas kernels: none -> 36.4 us  [the longest x1 31.5 us: shards(): pl.pallas_call(sections_kernel, out_shape=(jax.ShapeDtypeStruct(cells, F3...]
    all_gather x2 -> x0, blocking collectives: 23.3 us -> none  [the longest x1 12.4 us: shards(): lax.all_gather(low_share, 'pitch', axis=1, tiled=True)]
    ppermute x12 -> x0, waiting for transfers between devices: 6.95 us -> none  [the longest x6 5.65 us: padded_2(): lax.ppermute(lax.slice_in_dim(block, 0, width, axis=dim), axis, backward)]
    slice x12 -> x0, local copies, waits for them, and re-layouts: 5.58 us -> none  [the longest x3 1.97 us: shards(): radial_pad = jnp.pad(current, ((0, 0), (0, 0), (0, 0), (2, 2)), mode='edge')]
    sub x12 -> x0, other arithmetic: 5.46 us -> none  [the longest x9 4.7 us: face_sum(): 0.5 * (window(cell_flux, 1, faces_n) + window(cell_flux, 2, faces_n))]
    another operation x14 -> x0, other arithmetic: 3.94 us -> none  [the longest x3 2.24 us: shards(): return (current, jnp.stack([low_store, high_store]), ghosts)]
  transfers between devices with their start and end apart: 13 -> 0, of which waited for: 4 -> 0; matrix products, arithmetic and copies ran while one was open for 10% -> 0% of each run, Pallas kernels for 0% -> 0%
where the time goes in v1:
time: 42.2 us; the launch traced here: 41.9 us
  Pallas kernels  36.4 us (86%)
  local copies, waits for them, and re-layouts  4.87 us (12%)
  between operations  0.66 us (2%)
    pallas_call x1, Pallas kernels, shards(): pl.pallas_call(sections_kernel, out_shape=(jax.ShapeDtypeStruct(cells, F3...  31.5 us
    pallas_call x1, Pallas kernels, shards(): pl.pallas_call(store_kernel, out_shape=(jax.ShapeDtypeStruct(store_flat.s...  4.94 us
    unnamed x12, local copies, waits for them, and re-layouts  4.87 us

profile of v1, /device:TPU:1, one launch (start us, length us, event | category | flops | bytes accessed | tf_op | source)
XLA Modules:
  0.0 41.9 jit_solution(13721897336936351864)
XLA Ops:
  0.6 0.0 copy-start
  0.6 1.6 %copy-done = f32[2,49,10,4,128]{4,3,2,1,0:T(4,128)S(1)} copy-done((f32[2,49,10,4,128]{4,3,2,1,0:T(4,128)S(1)}, f32[2,49,10,4,128]{4,3,2,1,0:T(4,128)}, u32[]{:S(2)}) %copy-start) | copy-done | bytes 2007064
  2.2 0.0 copy-start.2
  2.2 1.0 %copy-done.2 = f32[5,8,16,128]{3,2,1,0:T(8,128)S(1)} copy-done((f32[5,8,16,128]{3,2,1,0:T(8,128)S(1)}, f32[5,8,16,128]{3,2,1,0:T(8,128)}, u32[]{:S(2)}) %copy-start.2) | copy-done | bytes 327704
  3.2 0.0 copy-start.3
  3.2 1.0 %copy-done.3 = f32[5,8,16,128]{3,2,1,0:T(8,128)S(1)} copy-done((f32[5,8,16,128]{3,2,1,0:T(8,128)S(1)}, f32[5,8,16,128]{3,2,1,0:T(8,128)}, u32[]{:S(2)}) %copy-start.3) | copy-done | bytes 327704
  4.1 0.0 copy-start.4
  4.1 0.7 %copy-done.4 = s32[2,4,128]{2,1,0:T(4,128)S(1)} copy-done((s32[2,4,128]{2,1,0:T(4,128)S(1)}, s32[2,4,128]{2,1,0:T(4,128)}, u32[]{:S(2)}) %copy-start.4) | copy-done | bytes 4120
  4.8 0.0 copy-start.5
  4.8 0.7 %copy-done.5 = s32[4,128]{1,0:T(4,128)S(1)} copy-done((s32[4,128]{1,0:T(4,128)S(1)}, s32[4,128]{1,0:T(4,128)}, u32[]{:S(2)}) %copy-start.5) | copy-done | bytes 2072
  5.5 0.0 copy-start.1
  5.5 31.5 %sections.1 = (f32[5,8,16,128]{3,2,1,0:T(8,128)S(1)}, f32[2,40,128]{2,1,0:T(8,128)S(1)}) custom-call(f32[5,8,16,128]{3,2,1,0:T(8,128)S(1)} %copy-done.2, f32[5,8,16,128]{3,2,1,0:T(8,128)S(1)} %copy-done.3, f32[2,49,40,128]{3,2,1,0:T(8,128)S(1)} %bitcast.3, s32[2,4,128]{2,1,0:T(4,128)S(1)} %copy-done.4, s32[4,128]{1,0:T(4,128)S(1)} %copy-done.5), custom_call_target="tpu_custom_call" | custom-call | tf_op jit(solution)/shard_map/sections/pallas_call | solution.py:520
  37.0 0.0 copy-done.1
  37.0 4.9 %store.1 = (f32[2,49,40,128]{3,2,1,0:T(8,128)}, f32[2,40,128]{2,1,0:T(8,128)}, f32[5,8,16,128]{3,2,1,0:T(8,128)}) custom-call(f32[2,49,40,128]{3,2,1,0:T(8,128)S(1)} %bitcast.4, s32[2,4,128]{2,1,0:T(4,128)S(1)} %copy-done.4, s32[4,128]{1,0:T(4,128)S(1)} %copy-done.5, f32[2,40,128]{2,1,0:T(8,128)S(1)} %get-tuple-element.8.samples, ...), custom_call_target="tpu_custom_call" | custom-call | tf_op jit(solution)/shard_map/store/pallas_call | solution.py:552
Async XLA Ops:
  0.6 1.6 %copy-start = (f32[2,49,10,4,128]{4,3,2,1,0:T(4,128)S(1)}, f32[2,49,10,4,128]{4,3,2,1,0:T(4,128)}, u32[]{:S(2)}) copy-start(f32[2,49,10,4,128]{4,3,2,1,0:T(4,128)} %param.7) | copy-start | bytes 6021124
  2.2 1.0 %copy-start.2 = (f32[5,8,16,128]{3,2,1,0:T(8,128)S(1)}, f32[5,8,16,128]{3,2,1,0:T(8,128)}, u32[]{:S(2)}) copy-start(f32[5,8,16,128]{3,2,1,0:T(8,128)} %flow_hbm.1) | copy-start | bytes 983044
  3.2 1.0 %copy-start.3 = (f32[5,8,16,128]{3,2,1,0:T(8,128)S(1)}, f32[5,8,16,128]{3,2,1,0:T(8,128)}, u32[]{:S(2)}) copy-start(f32[5,8,16,128]{3,2,1,0:T(8,128)} %prior_hbm.1) | copy-start | bytes 983044
  4.1 0.7 %copy-start.4 = (s32[2,4,128]{2,1,0:T(4,128)S(1)}, s32[2,4,128]{2,1,0:T(4,128)}, u32[]{:S(2)}) copy-start(s32[2,4,128]{2,1,0:T(4,128)} %times_ref.1) | copy-start | bytes 12292
  4.8 0.7 %copy-start.5 = (s32[4,128]{1,0:T(4,128)S(1)}, s32[4,128]{1,0:T(4,128)}, u32[]{:S(2)}) copy-start(s32[4,128]{1,0:T(4,128)} %harm_ref.1) | copy-start | bytes 6148
  5.5 31.5 %copy-start.1 = (f32[2,49,10,4,128]{4,3,2,1,0:T(4,128)S(1)}, f32[2,49,10,4,128]{4,3,2,1,0:T(4,128)}, u32[]{:S(2)}) copy-start(f32[2,49,10,4,128]{4,3,2,1,0:T(4,128)} %param.7) | copy-start | bytes 6021124

commit v2 on v1

--- a/solution.py
+++ b/solution.py
@@ -441,47 +441,32 @@
 
 
 def store_kernel(
-    store_hbm, times_ref, harm_ref, samples, state, store_out, ghosts_out, state_out,
-    store, fresh, in_sem, out_sem,
+    store, times_ref, harm_ref, samples, state, store_out, ghosts_out, state_out, fresh, out_sem
 ):
     per = HARM // GROUPS
-    fetch, write = {}, {}
-    for x in range(2):
-        for g in range(GROUPS):
-            for half in range(2):
-                at = 1 + HARM * half + per * g
-                rows, k = pl.ds(at, per), (x * GROUPS + g) * 2 + half
-                fetch[x, g, half] = pltpu.make_async_copy(
-                    store_hbm.at[x, rows], store.at[x, rows], in_sem.at[k]
-                )
-                write[x, g, half] = pltpu.make_async_copy(
-                    fresh.at[x, rows], store_out.at[x, rows], out_sem.at[k]
-                )
-        fetch[x, 0, 2] = pltpu.make_async_copy(
-            store_hbm.at[x, 0], store.at[x, 0], in_sem.at[4 * GROUPS + x]
+    state_copy = pltpu.make_async_copy(state, state_out, out_sem.at[0])
+    state_copy.start()
+    writes = [state_copy]
+
+    def write(x, first, count):
+        rows = pl.ds(first, count)
+        copy = pltpu.make_async_copy(
+            fresh.at[x, rows], store_out.at[x, rows], out_sem.at[len(writes)]
         )
-        write[x, 0, 2] = pltpu.make_async_copy(
-            fresh.at[x, 0], store_out.at[x, 0], out_sem.at[4 * GROUPS + x]
-        )
-    for x in range(2):
-        fetch[x, 0, 2].start()
-        for g in range(GROUPS):
-            for half in range(2):
-                fetch[x, g, half].start()
-    state_copy = pltpu.make_async_copy(state, state_out, out_sem.at[4 * GROUPS + 2])
-    state_copy.start()
+        copy.start()
+        writes.append(copy)
+
     count8 = twice(harm_ref)
     for x in range(2):
         turn = turned(base_turn(twice(times_ref.at[x])), PERIOD)
         lagged = turned(turn, LAG if x else -LAG)
         seen = tuple(samples[x, 8 * j : 8 * j + 8, :] for j in range(5))
-        fetch[x, 0, 2].wait()
         total = tuple(
             0.875 * store[x, 0, 8 * j : 8 * j + 8, :] + 0.125 * seen[j] for j in range(5)
         )
         for j in range(5):
             fresh[x, 0, 8 * j : 8 * j + 8, :] = total[j]
-        write[x, 0, 2].start()
+        write(x, 0, 1)
         carry = (turn, lagged, total)
 
         def harmonic(k, carry):
@@ -500,16 +485,13 @@
             return times_turn(now, turn), times_turn(late, lagged), tuple(sums)
 
         for g in range(GROUPS):
+            carry = lax.fori_loop(1 + per * g, 1 + per * (g + 1), harmonic, carry, unroll=2)
             for half in range(2):
-                fetch[x, g, half].wait()
-            carry = lax.fori_loop(1 + per * g, 1 + per * (g + 1), harmonic, carry)
-            for half in range(2):
-                write[x, g, half].start()
+                write(x, 1 + HARM * half + per * g, per)
         for j in range(5):
             ghosts_out[x, 8 * j : 8 * j + 8, :] = carry[2][j]
-    for copy in write.values():
+    for copy in writes:
         copy.wait()
-    state_copy.wait()
 
 
 def shards(flow_state, prior_state, fourier_store, sample_times, harmonics):
@@ -523,7 +505,7 @@
             jax.ShapeDtypeStruct(cells, F32),
             jax.ShapeDtypeStruct((2, 40, 128), F32),
         ),
-        in_specs=[anywhere] * 5,
+        in_specs=[pl.BlockSpec(memory_space=pltpu.HBM)] * 5,
         out_specs=(vmem, vmem),
         scratch_shapes=[
             pltpu.VMEM((5, 12, 32, 128), F32),
@@ -548,7 +530,7 @@
             collective_id=0, has_side_effects=True, vmem_limit_bytes=24 * 1024 * 1024
         ),
         name="sections",
-    )(flow_state, prior_state, store_flat, sample_times, harmonics)
+    )(*[pltpu.with_memory_space_constraint(x, pltpu.HBM) for x in (flow_state, prior_state, store_flat, sample_times, harmonics)])
     new_store, ghosts, new_state = pl.pallas_call(
         store_kernel,
         out_shape=(
@@ -556,12 +538,10 @@
             jax.ShapeDtypeStruct((2, 40, 128), F32),
             jax.ShapeDtypeStruct(cells, F32),
         ),
-        in_specs=[anywhere, vmem, vmem, vmem, vmem],
+        in_specs=[vmem, vmem, vmem, vmem, anywhere],
         out_specs=(anywhere, vmem, anywhere),
         scratch_shapes=[
             pltpu.VMEM((2, COEFS, 40, 128), F32),
-            pltpu.VMEM((2, COEFS, 40, 128), F32),
-            pltpu.SemaphoreType.DMA((4 * GROUPS + 2,)),
             pltpu.SemaphoreType.DMA((4 * GROUPS + 3,)),
         ],
         compiler_params=pltpu.CompilerParams(vmem_limit_bytes=24 * 1024 * 1024),

time: 42.2 us -> 34.7 us (0.82)
  the two profiles are of different devices: /device:TPU:1 before, /device:TPU:33 now
where the time goes in v2:
time: 34.7 us; the launch traced here: 34.6 us
  Pallas kernels  33.9 us (98%)
  between operations  0.69 us (2%)
    pallas_call x1, Pallas kernels, shards(): pl.pallas_call(sections_kernel, out_shape=(jax.ShapeDtypeStruct(cells, F3...  31.7 us
    pallas_call x1, Pallas kernels, shards(): pl.pallas_call(store_kernel, out_shape=(jax.ShapeDtypeStruct(store_flat.s...  2.16 us

profile of v2, /device:TPU:33, one launch (start us, length us, event | category | flops | bytes accessed | tf_op | source)
XLA Modules:
  0.0 34.6 jit_solution(12296961655593474803)
XLA Ops:
  0.6 0.0 copy-start.2
  0.6 0.0 copy-start.1
  0.7 0.0 copy-start
  0.7 31.7 %sections.1 = (f32[5,8,16,128]{3,2,1,0:T(8,128)S(1)}, f32[2,40,128]{2,1,0:T(8,128)S(1)}) custom-call(f32[5,8,16,128]{3,2,1,0:T(8,128)} %flow_hbm.1, f32[5,8,16,128]{3,2,1,0:T(8,128)} %prior_hbm.1, f32[2,49,40,128]{3,2,1,0:T(8,128)} %bitcast.3, s32[2,4,128]{2,1,0:T(4,128)} %times_ref.1, s32[4,128]{1,0:T(4,128)} %harm_ref.1), custom_call_target="tpu_custom_call" | custom-call | tf_op jit(solution)/shard_map/sections/pallas_call | solution.py:502
  32.4 0.0 copy-done.2
  32.4 0.0 copy-done.1
  32.4 0.0 copy-done
  32.4 2.2 %store.1 = (f32[2,49,40,128]{3,2,1,0:T(8,128)}, f32[2,40,128]{2,1,0:T(8,128)}, f32[5,8,16,128]{3,2,1,0:T(8,128)}) custom-call(f32[2,49,40,128]{3,2,1,0:T(8,128)S(1)} %bitcast.4, s32[2,4,128]{2,1,0:T(4,128)S(1)} %copy-done.1, s32[4,128]{1,0:T(4,128)S(1)} %copy-done.2, f32[2,40,128]{2,1,0:T(8,128)S(1)} %get-tuple-element.8.samples, ...), custom_call_target="tpu_custom_call" | custom-call | tf_op jit(solution)/shard_map/store/pallas_call | solution.py:534
Async XLA Ops:
  0.6 31.7 %copy-start.2 = (s32[4,128]{1,0:T(4,128)S(1)}, s32[4,128]{1,0:T(4,128)}, u32[]{:S(2)}) copy-start(s32[4,128]{1,0:T(4,128)} %harm_ref.1) | copy-start | bytes 6148
  0.6 31.7 %copy-start.1 = (s32[2,4,128]{2,1,0:T(4,128)S(1)}, s32[2,4,128]{2,1,0:T(4,128)}, u32[]{:S(2)}) copy-start(s32[2,4,128]{2,1,0:T(4,128)} %times_ref.1) | copy-start | bytes 12292
  0.7 31.7 %copy-start = (f32[2,49,10,4,128]{4,3,2,1,0:T(4,128)S(1)}, f32[2,49,10,4,128]{4,3,2,1,0:T(4,128)}, u32[]{:S(2)}) copy-start(f32[2,49,10,4,128]{4,3,2,1,0:T(4,128)} %param.7) | copy-start | bytes 6021124

commit v3 on v2

v3 whole, which is shorter than its diff:
```python
import functools
import math

import jax
import jax.numpy as jnp
from jax import lax
from jax.experimental import pallas as pl
from jax.experimental.pallas import tpu as pltpu
from jax.sharding import PartitionSpec as P

MESH = pl.DeviceIdType.MESH
F32 = jnp.float32
NT = 96
HARM = 24
COEFS = 2 * HARM + 1
PERIOD = 2.0 * math.pi / NT
LAG = 2.0 * math.pi * 0.3
SECTIONS = (1.0 / 3.0, 0.5, 1.0)
CENTER = (8, 16)
EXTENDED = (4, 12, 20)


def twice(ref):
    rows = ref[...]
    return jnp.concatenate([rows, rows], axis=0)


def base_turn(times):
    quarter = (times - NT // 2).astype(F32) * (PERIOD / 4.0)
    sq = quarter * quarter
    s = quarter * (1.0 + sq * (-1.0 / 6 + sq * (1.0 / 120 + sq * (-1.0 / 5040 + sq * (1.0 / 362880)))))
    c = 1.0 + sq * (
        -0.5 + sq * (1.0 / 24 + sq * (-1.0 / 720 + sq * (1.0 / 40320 + sq * (-1.0 / 3628800))))
    )
    for _ in range(2):
        c, s = 1.0 - 2.0 * s * s, 2.0 * s * c
    return -c, -s


def turned(turn, angle):
    c, s = turn
    ca, sa = math.cos(angle), math.sin(angle)
    return c * ca - s * sa, s * ca + c * sa


def times_turn(a, b):
    return a[0] * b[0] - a[1] * b[1], a[1] * b[0] + a[0] * b[1]


def half_flux(cell, direction):
    rho, mp, ma, mr, energy = cell
    inv = pl.reciprocal(rho, approx=True)
    half_inv = inv * (1.0 - (0.5 * rho) * inv)
    kinetic = (mp * mp + ma * ma + mr * mr) * half_inv
    half_p = 0.2 * (energy - kinetic)
    moment = cell[direction]
    half_u = moment * half_inv
    parts = [
        0.5 * moment,
        mp * half_u,
        ma * half_u,
        mr * half_u,
        (energy + (half_p + half_p)) * half_u,
    ]
    parts[direction] = parts[direction] + half_p
    return parts


def section(s, cur, flow, prior, out, out_offsets, first, count, rows):
    step = 0.1 * SECTIONS[s]
    lane = lax.broadcasted_iota(jnp.int32, (8, 128), 1)
    at_low, at_high = lane == 0, lane == 127

    def after(x):
        return jnp.where(at_high, x, pltpu.roll(x, 127, 1))

    def before(x):
        return jnp.where(at_low, x, pltpu.roll(x, 1, 1))

    def layer(i, carry):
        at = first + i
        li = at + 2
        for r0 in rows:

            def load(dl, dr):
                return [cur[v, li + dl, pl.ds(r0 + dr, 8), :] for v in range(5)]

            mid = load(0, 0)
            near = [load(1, 0), load(-1, 0), load(0, 1), load(0, -1)]
            far = [load(2, 0), load(-2, 0), load(0, 2), load(0, -2)]
            fluxes = [half_flux(near[k], 1 + k // 2) for k in range(4)]
            radial = half_flux(mid, 3)
            for v in range(5):
                total = (fluxes[0][v] - fluxes[1][v]) + (fluxes[2][v] - fluxes[3][v])
                n1 = (near[0][v] + near[1][v]) + (near[2][v] + near[3][v])
                n2 = (far[0][v] + far[1][v]) + (far[2][v] + far[3][v])
                x = mid[v]
                eighth = 0.125 * x
                up = (eighth + radial[v]) - 0.03125 * after(x)
                down = (eighth - radial[v]) - 0.03125 * before(x)
                total = total + (after(up) + before(down)) + (0.125 * n1 - 0.03125 * n2)
                base = (1.0 + 8.0 * step) * flow[v, li, pl.ds(r0, 8), :] - (
                    2.0 * step
                ) * prior[v, at, pl.ds(r0, 8), :]
                new = base - (6.0 - 0.5625) * step * x - step * total
                out[v, at + out_offsets[0], pl.ds(r0 + out_offsets[1], 8), :] = new
        return carry

    lax.fori_loop(0, count, layer, 0)


def sections_kernel(
    flow_hbm, prior_hbm, store_hbm, times_hbm, harm_hbm,
    state_out, samples_out,
    u0, u1, u2, prior, store, times, harm, share, ghosts, relay, faces, samples,
    local_sem, send_sem, recv_sem, word_sem,
):
    p = lax.axis_index("pitch")
    b = lax.axis_index("blk")
    n_blk = lax.axis_size("blk")
    last = lax.axis_size("pitch") - 1
    first_p, last_p = p == 0, p == last
    not_first, not_last = p > 0, p < last
    is_end = jnp.logical_or(first_p, last_p)
    b_low, b_high = b > 0, b < n_blk - 1
    above, below = {"pitch": p + 1}, {"pitch": p - 1}
    states = (u0, u1, u2)
    both = jnp.logical_and

    def signal(sem, where, cond):
        @pl.when(cond)
        def _():
            pl.semaphore_signal(sem, inc=1, device_id=where, device_id_type=MESH)

    def await_word(k, cond):
        @pl.when(cond)
        def _():
            pl.semaphore_wait(word_sem.at[k], 1)

    def number(cond):
        return cond.astype(jnp.int32)

    barrier = pltpu.get_barrier_semaphore()
    signal(barrier, above, not_last)
    signal(barrier, {"blk": b - 1}, b_low)
    signal(barrier, {"blk": b + 1}, b_high)
    signal(barrier, {"pitch": last}, first_p)
    signal(barrier, {"blk": b - 1, "pitch": last}, both(first_p, b_low))

    loads = [
        pltpu.make_async_copy(flow_hbm, u0.at[:, 2:10, 8:24, :], local_sem.at[0]),
        pltpu.make_async_copy(store_hbm.at[0], store.at[0], local_sem.at[1]),
        pltpu.make_async_copy(store_hbm.at[1], store.at[1], local_sem.at[2]),
        pltpu.make_async_copy(prior_hbm, prior.at[:, :, 8:24, :], local_sem.at[3]),
        pltpu.make_async_copy(times_hbm, times, local_sem.at[4]),
        pltpu.make_async_copy(harm_hbm, harm, local_sem.at[5]),
    ]
    for k in (0, 4, 5, 1, 2, 3):
        loads[k].start()

    pl.semaphore_wait(
        barrier,
        number(not_first) + number(b_low) + number(b_high)
        + number(last_p) * (1 + number(b_high)),
    )
    signal(word_sem.at[0], below, not_first)
    signal(word_sem.at[1], {"pitch": 0}, last_p)

    sent = []

    def remote(src, dst, where, send_if, recv_if):
        k = len(sent)
        copy = pltpu.make_async_remote_copy(
            src_ref=src,
            dst_ref=dst,
            send_sem=send_sem.at[k],
            recv_sem=recv_sem.at[k],
            device_id=where,
            device_id_type=MESH,
        )
        sent.append((copy, send_if))
        return copy, send_if, recv_if

    def send(*copies):
        for copy, send_if, _ in copies:

            @pl.when(send_if)
            def _():
                copy.start()

    def arrive(*copies):
        for copy, _, recv_if in copies:

            @pl.when(recv_if)
            def _():
                copy.wait_recv()

    chunk_low = [lax.rem(b + t, 2) == 0 for t in range(2)]
    chunk_row = [pl.multiple_of(jnp.where(low, 8, 16), 8) for low in chunk_low]

    def pitch_copies(src, layer, shift, target):
        made = []
        for row in chunk_row:
            rows, there = pl.ds(pl.multiple_of(row - shift, 8), 8), pl.ds(row, 8)
            made.append(
                (
                    remote(
                        src.at[:, layer + 6 : layer + 8, rows, :], target.at[:, 0:2, there, :],
                        above, not_last, not_first,
                    ),
                    remote(
                        src.at[:, layer : layer + 2, rows, :], target.at[:, 10:12, there, :],
                        below, not_first, not_last,
                    ),
                )
            )
        return made

    pitch = [pitch_copies(flow_hbm, 0, 8, u0), pitch_copies(u1, 2, 0, u1), pitch_copies(u2, 2, 0, u2)]
    send(pitch[0][0][1], pitch[0][1][1])

    g6 = jnp.where(first_p, 0, 2)
    g4 = jnp.where(first_p, 0, 4)

    def beside(src, source, target, layers, count, shift, rows, cond, skip=0):
        there = pl.ds(layers + shift, count)
        here = pl.ds(layers + source[2], count)
        low, high = source[0], source[1]
        return (
            remote(
                src.at[:, here, high - skip - rows : high - skip, :],
                target.at[:, there, 8 - skip - rows : 8 - skip, :],
                {"blk": b + 1}, both(cond, b_high), both(cond, b_low),
            ),
            remote(
                src.at[:, here, low + skip : low + skip + rows, :],
                target.at[:, there, 24 + skip : 24 + skip + rows, :],
                {"blk": b - 1}, both(cond, b_low), both(cond, b_high),
            ),
        )

    plain, padded = (0, 16, 0), (8, 24, 2)
    flow_sides = beside(flow_hbm, plain, u0, 0, 8, 2, 2, p >= 0)
    flow_more = beside(flow_hbm, plain, u0, g6, 6, 2, 4, is_end, 2)
    prior_sides = beside(prior_hbm, plain, prior, g4, 4, 0, 4, is_end)
    send(*flow_sides)

    def exchanged(s, q):
        ends = [0] if s == 1 else [0, 1]
        skip_first = both(first_p, jnp.asarray(q in ends))
        skip_last = both(last_p, jnp.asarray(3 - q in ends))
        return jnp.logical_not(jnp.logical_or(skip_first, skip_last))

    axial = {
        (s, q): beside(states[s], padded, states[s], 2 * q, 2, 2, 2, exchanged(s, q))
        for s in (1, 2)
        for q in range(4)
    }

    def outer_sides(s, t, wait):
        for q in (0, 3):
            to_above, to_below = axial[s, q]
            for low in (True, False):
                copy, send_if, recv_if = to_below if low != wait else to_above
                cond = both(recv_if if wait else send_if, chunk_low[t] == low)

                @pl.when(cond)
                def _():
                    copy.wait_recv() if wait else copy.start()

    for k in (4, 5):
        loads[k].wait()
    count8 = twice(harm)
    for x in range(2):
        loads[1 + x].wait()
        turn = turned(base_turn(twice(times.at[x])), LAG if x else -LAG)

        def harmonic(k, carry):
            now, total = carry
            keep = k <= count8
            c, s = jnp.where(keep, now[0], 0.0), jnp.where(keep, now[1], 0.0)
            total = tuple(
                total[j]
                + (
                    store[x, k, 8 * j : 8 * j + 8, :] * c
                    + store[x, HARM + k, 8 * j : 8 * j + 8, :] * s
                )
                for j in range(5)
            )
            return times_turn(now, turn), total

        start = tuple(store[x, 0, 8 * j : 8 * j + 8, :] for j in range(5))
        _, total = lax.fori_loop(1, HARM + 1, harmonic, (turn, start))
        for j in range(5):
            share[x, 8 * j : 8 * j + 8, :] = total[j]

    low_early = [
        remote(share.at[0], ghosts.at[2], {"pitch": 0}, p == 1, first_p),
        remote(share.at[0], ghosts.at[4], {"pitch": 0}, last_p, first_p),
        remote(
            share.at[0], ghosts.at[0], {"blk": b + 1, "pitch": 0},
            both(last_p, b_high), both(first_p, b_low),
        ),
        remote(
            share.at[0], ghosts.at[5], {"blk": b - 1, "pitch": 0},
            both(first_p, b_low), both(first_p, b_high),
        ),
    ]
    low_later = remote(share.at[0], ghosts.at[3], {"pitch": 0}, p == 2, first_p)
    relayed = remote(share.at[1], relay.at[1], {"pitch": 0}, p == 1, first_p)
    high_early = remote(
        share.at[1], ghosts.at[0], {"blk": b + 1, "pitch": last},
        both(last_p, b_high), both(last_p, b_low),
    )
    high_next = remote(share.at[1], ghosts.at[3], {"pitch": last}, p == 2, last_p)
    high_relay = remote(relay, ghosts.at[1:3], {"pitch": last}, first_p, last_p)
    high_beside = remote(
        share.at[1], ghosts.at[5], {"blk": b - 1, "pitch": last},
        both(first_p, b_low), both(last_p, b_high),
    )
    send(*low_early, relayed, high_early, *flow_more, *prior_sides)

    await_word(0, not_last)
    send(pitch[0][0][0], pitch[0][1][0])
    signal(word_sem.at[2], above, jnp.logical_or(p == 1, p == 2))
    send(high_next)
    await_word(2, p == 2)
    send(low_later)

    def fill_edges(s, first, count):
        ref = states[s]
        for cond, row, source in ((b == 0, 6, 8), (b == n_blk - 1, 24, 23)):

            @pl.when(cond)
            def _():
                def layer(i, carry):
                    for v in range(5):
                        edge = ref[v, 2 + first + i, source : source + 1, :]
                        ref[v, 2 + first + i, row : row + 2, :] = jnp.broadcast_to(edge, (2, 128))
                    return carry

                lax.fori_loop(0, count, layer, 0)

    def update(s, first, count, rows):
        if s < 2:
            section(s, states[s], u0, prior, states[s + 1], (2, 0), first, count, rows)
        else:
            section(s, states[s], u0, prior, state_out, (0, -8), first, count, rows)

    def all_layers(s, between=None):
        fill_edges(s, 0, 8)
        for t in range(2):
            if s > 0:
                outer_sides(s, t, True)
            for side, cond, first in ((0, not_first, 0), (1, not_last, 6)):

                @pl.when(cond)
                def _():
                    pitch[s][t][side][0].wait_recv()
                    update(s, first, 2, (chunk_row[t],))
                    if s < 2:
                        pitch[s + 1][t][1 - side][0].start()

            if s < 2:
                outer_sides(s + 1, t, False)
            if t == 0:
                if s > 0:
                    arrive(*axial[s, 1], *axial[s, 2])
                if s == 1:
                    m2 = jnp.where(first_p, 4, 2)
                    update(s, jnp.where(is_end, m2, 2), jnp.where(is_end, 2, 4), CENTER)
                else:
                    update(s, 2, 4, CENTER)
                if s < 2:
                    send(*axial[s + 1, 1], *axial[s + 1, 2])
                if between:
                    between()

    loads[0].wait()
    loads[3].wait()
    arrive(*flow_sides)
    all_layers(0)

    @pl.when(first_p)
    def _():
        pl.semaphore_wait(word_sem.at[1], 1)
        relay[0] = share[1]
        relayed[0].wait_recv()
        high_relay[0].start()

    send(high_beside)
    face_copies = []
    for x, source in ((0, 3), (1, 0)):
        for j in range(4):
            if j != source:
                face_copies.append(
                    remote(faces.at[j], samples.at[x], {"pitch": j}, p == source, p == j)
                )

    def ghosts_chain():
        @pl.when(is_end)
        def _():
            arrive(*flow_more, *prior_sides, *low_early, low_later, high_early, high_next, high_relay, high_beside)
            pl.when(first_p)(lambda: ghosts.__setitem__(1, share[0]))
            pl.when(last_p)(lambda: ghosts.__setitem__(4, share[1]))
            outside = jnp.where(first_p, 0, 10)
            for k in range(6):

                @pl.when(b_low if k == 0 else (b_high if k == 5 else is_end))
                def _():
                    for v in range(5):
                        for layer in range(2):
                            at = (2 * v + layer) * 4
                            block = ghosts[k, at : at + 4, :]
                            for ref in states:
                                ref[v, outside + layer, 4 + 4 * k : 8 + 4 * k, :] = block

            for q, mine in ((1, first_p), (2, last_p)):
                for copy, send_if, _ in axial[1, q]:

                    @pl.when(both(send_if, mine))
                    def _():
                        copy.wait_send()

            near = jnp.where(first_p, 0, 6)
            update(0, g4, 4, EXTENDED)
            fill_edges(1, g4, 4)
            update(1, g4, 4, EXTENDED)
            fill_edges(2, g4, 4)
            update(2, near, 2, CENTER)
            for j in range(4):
                for v in range(5):
                    for layer in range(2):
                        at = (2 * v + layer) * 4
                        faces[j, at : at + 4, :] = state_out[v, near + layer, 4 * j : 4 * j + 4, :]

        await_word(2, last_p)
        send(*face_copies)
        pl.when(first_p)(lambda: samples.__setitem__(1, faces[0]))
        pl.when(last_p)(lambda: samples.__setitem__(0, faces[3]))

    all_layers(1, ghosts_chain)
    all_layers(2)
    arrive(*face_copies)
    samples_out[...] = samples[...]
    early = [(axial[1, 1], first_p), (axial[1, 2], last_p)]
    for copy, cond in sent:
        for copies, mine in early:
            if any(copy is made[0] for made in copies):
                cond = both(cond, jnp.logical_not(mine))

        @pl.when(cond)
        def _():
            copy.wait_send()


GROUPS = 4


def store_kernel(
    store, times_ref, harm_ref, samples, state, store_out, ghosts_out, state_out, fresh, out_sem
):
    per = HARM // GROUPS
    state_copy = pltpu.make_async_copy(state, state_out, out_sem.at[0])
    state_copy.start()
    writes = [state_copy]

    def write(x, first, count):
        rows = pl.ds(first, count)
        copy = pltpu.make_async_copy(
            fresh.at[x, rows], store_out.at[x, rows], out_sem.at[len(writes)]
        )
        copy.start()
        writes.append(copy)

    count8 = twice(harm_ref)
    for x in range(2):
        turn = turned(base_turn(twice(times_ref.at[x])), PERIOD)
        lagged = turned(turn, LAG if x else -LAG)
        seen = tuple(samples[x, 8 * j : 8 * j + 8, :] for j in range(5))
        total = tuple(
            0.875 * store[x, 0, 8 * j : 8 * j + 8, :] + 0.125 * seen[j] for j in range(5)
        )
        for j in range(5):
            fresh[x, 0, 8 * j : 8 * j + 8, :] = total[j]
        write(x, 0, 1)
        carry = (turn, lagged, total)

        def harmonic(k, carry):
            now, late, total = carry
            keep = k <= count8
            c, s = jnp.where(keep, late[0], 0.0), jnp.where(keep, late[1], 0.0)
            wc, ws = 0.25 * now[0], 0.25 * now[1]
            sums = []
            for j in range(5):
                rows = slice(8 * j, 8 * j + 8)
                new_c = 0.875 * store[x, k, rows, :] + wc * seen[j]
                new_s = 0.875 * store[x, HARM + k, rows, :] + ws * seen[j]
                fresh[x, k, rows, :] = new_c
                fresh[x, HARM + k, rows, :] = new_s
                sums.append(total[j] + (new_c * c + new_s * s))
            return times_turn(now, turn), times_turn(late, lagged), tuple(sums)

        for g in range(GROUPS):
            carry = lax.fori_loop(1 + per * g, 1 + per * (g + 1), harmonic, carry, unroll=2)
            for half in range(2):
                write(x, 1 + HARM * half + per * g, per)
        for j in range(5):
            ghosts_out[x, 8 * j : 8 * j + 8, :] = carry[2][j]
    for copy in writes:
        copy.wait()


def shards(flow_state, prior_state, fourier_store, sample_times, harmonics):
    cells = flow_state.shape
    store_flat = fourier_store.reshape(2, COEFS, 40, 128)
    anywhere = pl.BlockSpec(memory_space=pl.ANY)
    vmem = pl.BlockSpec(memory_space=pltpu.VMEM)
    state, samples = pl.pallas_call(
        sections_kernel,
        out_shape=(
            jax.ShapeDtypeStruct(cells, F32),
            jax.ShapeDtypeStruct((2, 40, 128), F32),
        ),
        in_specs=[pl.BlockSpec(memory_space=pltpu.HBM)] * 5,
        out_specs=(vmem, vmem),
        scratch_shapes=[
            pltpu.VMEM((5, 12, 32, 128), F32),
            pltpu.VMEM((5, 12, 32, 128), F32),
            pltpu.VMEM((5, 12, 32, 128), F32),
            pltpu.VMEM((5, 8, 32, 128), F32),
            pltpu.VMEM((2, COEFS, 40, 128), F32),
            pltpu.VMEM((2, 4, 128), jnp.int32),
            pltpu.VMEM((4, 128), jnp.int32),
            pltpu.VMEM((2, 40, 128), F32),
            pltpu.VMEM((6, 40, 128), F32),
            pltpu.VMEM((2, 40, 128), F32),
            pltpu.VMEM((4, 40, 128), F32),
            pltpu.VMEM((2, 40, 128), F32),
            pltpu.SemaphoreType.DMA((6,)),
            pltpu.SemaphoreType.DMA((64,)),
            pltpu.SemaphoreType.DMA((64,)),
            pltpu.SemaphoreType.REGULAR((3,)),
        ],
        compiler_params=pltpu.CompilerParams(
            collective_id=0, has_side_effects=True, vmem_limit_bytes=24 * 1024 * 1024
        ),
        name="sections",
    )(*[pltpu.with_memory_space_constraint(x, pltpu.HBM) for x in (flow_state, prior_state, store_flat, sample_times, harmonics)])
    new_store, ghosts, new_state = pl.pallas_call(
        store_kernel,
        out_shape=(
            jax.ShapeDtypeStruct(store_flat.shape, F32),
            jax.ShapeDtypeStruct((2, 40, 128), F32),
            jax.ShapeDtypeStruct(cells, F32),
        ),
        in_specs=[vmem, vmem, vmem, vmem, anywhere],
        out_specs=(anywhere, vmem, anywhere),
        scratch_shapes=[
            pltpu.VMEM((2, COEFS, 40, 128), F32),
            pltpu.SemaphoreType.DMA((4 * GROUPS + 3,)),
        ],
        compiler_params=pltpu.CompilerParams(vmem_limit_bytes=24 * 1024 * 1024),
        name="store",
    )(store_flat, sample_times, harmonics, samples, state)
    return (
        new_state,
        new_store.reshape(fourier_store.shape),
        ghosts.reshape(2, 10, 4, 128),
    )


def solution(mesh):
    placed = (
        P(None, "pitch", "blk", None),
        P(None, "pitch", "blk", None),
        P(None, None, None, ("blk", "pitch"), None),
        P(None, ("blk", "pitch"), None),
        P(("blk", "pitch"), None),
    )
    return jax.shard_map(
        shards,
        mesh=mesh,
        in_specs=placed,
        out_specs=(
            P(None, "pitch", "blk", None),
            P(None, None, None, ("blk", "pitch"), None),
            P(None, None, ("blk", "pitch"), None),
        ),
        check_vma=False,
    )
```

time: 34.7 us -> 33.3 us (0.960)
  the two profiles are of different devices: /device:TPU:33 before, /device:TPU:24 now
where the time goes in v3:
time: 33.3 us; the launch traced here: 33.2 us
  Pallas kernels  32.5 us (98%)
  between operations  0.69 us (2%)
    pallas_call x1, Pallas kernels, shards(): pl.pallas_call(sections_kernel, out_shape=(jax.ShapeDtypeStruct(cells, F3...  30.4 us
    pallas_call x1, Pallas kernels, shards(): pl.pallas_call(store_kernel, out_shape=(jax.ShapeDtypeStruct(store_flat.s...  2.16 us

profile of v3, /device:TPU:24, one launch (start us, length us, event | category | flops | bytes accessed | tf_op | source)
XLA Modules:
  0.0 33.2 jit_solution(8395467421789667000)
XLA Ops:
  0.6 0.0 copy-start.2
  0.6 0.0 copy-start.1
  0.7 0.0 copy-start
  0.7 30.4 %sections.1 = (f32[5,8,16,128]{3,2,1,0:T(8,128)S(1)}, f32[2,40,128]{2,1,0:T(8,128)S(1)}) custom-call(f32[5,8,16,128]{3,2,1,0:T(8,128)} %flow_hbm.1, f32[5,8,16,128]{3,2,1,0:T(8,128)} %prior_hbm.1, f32[2,49,40,128]{3,2,1,0:T(8,128)} %bitcast.3, s32[2,4,128]{2,1,0:T(4,128)} %times_ref.1, s32[4,128]{1,0:T(4,128)} %harm_ref.1), custom_call_target="tpu_custom_call" | custom-call | tf_op jit(solution)/shard_map/sections/pallas_call | solution.py:519
  31.0 0.0 copy-done.2
  31.0 0.0 copy-done.1
  31.1 0.0 copy-done
  31.1 2.2 %store.1 = (f32[2,49,40,128]{3,2,1,0:T(8,128)}, f32[2,40,128]{2,1,0:T(8,128)}, f32[5,8,16,128]{3,2,1,0:T(8,128)}) custom-call(f32[2,49,40,128]{3,2,1,0:T(8,128)S(1)} %bitcast.4, s32[2,4,128]{2,1,0:T(4,128)S(1)} %copy-done.1, s32[4,128]{1,0:T(4,128)S(1)} %copy-done.2, f32[2,40,128]{2,1,0:T(8,128)S(1)} %get-tuple-element.8.samples, ...), custom_call_target="tpu_custom_call" | custom-call | tf_op jit(solution)/shard_map/store/pallas_call | solution.py:550
Async XLA Ops:
  0.6 30.4 %copy-start.2 = (s32[4,128]{1,0:T(4,128)S(1)}, s32[4,128]{1,0:T(4,128)}, u32[]{:S(2)}) copy-start(s32[4,128]{1,0:T(4,128)} %harm_ref.1) | copy-start | bytes 6148
  0.6 30.4 %copy-start.1 = (s32[2,4,128]{2,1,0:T(4,128)S(1)}, s32[2,4,128]{2,1,0:T(4,128)}, u32[]{:S(2)}) copy-start(s32[2,4,128]{2,1,0:T(4,128)} %times_ref.1) | copy-start | bytes 12292
  0.7 30.4 %copy-start = (f32[2,49,10,4,128]{4,3,2,1,0:T(4,128)S(1)}, f32[2,49,10,4,128]{4,3,2,1,0:T(4,128)}, u32[]{:S(2)}) copy-start(f32[2,49,10,4,128]{4,3,2,1,0:T(4,128)} %param.7) | copy-start | bytes 6021124

commit v4 on v3

--- a/solution.py
+++ b/solution.py
@@ -106,12 +106,15 @@
                 out[v, at + out_offsets[0], pl.ds(r0 + out_offsets[1], 8), :] = new
         return carry
 
-    lax.fori_loop(0, count, layer, 0)
+    if isinstance(count, int) and count == 2 and len(rows) == 1:
+        lax.fori_loop(0, count, layer, 0, unroll=True)
+    else:
+        lax.fori_loop(0, count, layer, 0)
 
 
 def sections_kernel(
     flow_hbm, prior_hbm, store_hbm, times_hbm, harm_hbm,
-    state_out, samples_out,
+    state_out, store_out, ghosts_out,
     u0, u1, u2, prior, store, times, harm, share, ghosts, relay, faces, samples,
     local_sem, send_sem, recv_sem, word_sem,
 ):
@@ -155,7 +158,7 @@
         pltpu.make_async_copy(times_hbm, times, local_sem.at[4]),
         pltpu.make_async_copy(harm_hbm, harm, local_sem.at[5]),
     ]
-    for k in (0, 4, 5, 1, 2, 3):
+    for k in (0, 4, 5):
         loads[k].start()
 
     pl.semaphore_wait(
@@ -244,6 +247,8 @@
     flow_more = beside(flow_hbm, plain, u0, g6, 6, 2, 4, is_end, 2)
     prior_sides = beside(prior_hbm, plain, prior, g4, 4, 0, 4, is_end)
     send(*flow_sides)
+    for k in (1, 2, 3):
+        loads[k].start()
 
     def exchanged(s, q):
         ends = [0] if s == 1 else [0, 1]
@@ -257,8 +262,8 @@
         for q in range(4)
     }
 
-    def outer_sides(s, t, wait):
-        for q in (0, 3):
+    def outer_sides(s, t, wait, layers=(0, 3)):
+        for q in layers:
             to_above, to_below = axial[s, q]
             for low in (True, False):
                 copy, send_if, recv_if = to_below if low != wait else to_above
@@ -349,6 +354,9 @@
 
     def all_layers(s, between=None):
         fill_edges(s, 0, 8)
+        if s == 0:
+            update(0, 2, 4, CENTER)
+            send(*axial[1, 1], *axial[1, 2])
         for t in range(2):
             if s > 0:
                 outer_sides(s, t, True)
@@ -361,10 +369,12 @@
                     if s < 2:
                         pitch[s + 1][t][1 - side][0].start()
 
-            if s < 2:
-                outer_sides(s + 1, t, False)
-            if t == 0:
-                if s > 0:
+                if s < 2:
+                    outer_sides(s + 1, t, False, (3 * side,))
+            if t == 0 and between:
+                between()
+            if t == 0 and s > 0:
+                if s == 2:
                     arrive(*axial[s, 1], *axial[s, 2])
                 if s == 1:
                     m2 = jnp.where(first_p, 4, 2)
@@ -373,8 +383,6 @@
                     update(s, 2, 4, CENTER)
                 if s < 2:
                     send(*axial[s + 1, 1], *axial[s + 1, 2])
-                if between:
-                    between()
 
     loads[0].wait()
     loads[3].wait()
@@ -439,10 +447,41 @@
         pl.when(first_p)(lambda: samples.__setitem__(1, faces[0]))
         pl.when(last_p)(lambda: samples.__setitem__(0, faces[3]))
 
-    all_layers(1, ghosts_chain)
-    all_layers(2)
-    arrive(*face_copies)
-    samples_out[...] = samples[...]
+    arrive(*axial[1, 1], *axial[1, 2])
+    ghosts_chain()
+    all_layers(1)
+    def refresh():
+        arrive(*face_copies)
+        for x in range(2):
+            turn = turned(base_turn(twice(times.at[x])), PERIOD)
+            lagged = turned(turn, LAG if x else -LAG)
+            seen = tuple(samples[x, 8 * j : 8 * j + 8, :] for j in range(5))
+            total = tuple(
+                0.875 * store[x, 0, 8 * j : 8 * j + 8, :] + 0.125 * seen[j] for j in range(5)
+            )
+            for j in range(5):
+                store_out[x, 0, 8 * j : 8 * j + 8, :] = total[j]
+
+            def harmonic(k, carry):
+                now, late, total = carry
+                keep = k <= count8
+                c, s = jnp.where(keep, late[0], 0.0), jnp.where(keep, late[1], 0.0)
+                wc, ws = 0.25 * now[0], 0.25 * now[1]
+                sums = []
+                for j in range(5):
+                    rows = slice(8 * j, 8 * j + 8)
+                    new_c = 0.875 * store[x, k, rows, :] + wc * seen[j]
+                    new_s = 0.875 * store[x, HARM + k, rows, :] + ws * seen[j]
+                    store_out[x, k, rows, :] = new_c
+                    store_out[x, HARM + k, rows, :] = new_s
+                    sums.append(total[j] + (new_c * c + new_s * s))
+                return times_turn(now, turn), times_turn(late, lagged), tuple(sums)
+
+            carry = lax.fori_loop(1, HARM + 1, harmonic, (turn, lagged, total), unroll=2)
+            for j in range(5):
+                ghosts_out[x, 8 * j : 8 * j + 8, :] = carry[2][j]
+
+    all_layers(2, refresh)
     early = [(axial[1, 1], first_p), (axial[1, 2], last_p)]
     for copy, cond in sent:
         for copies, mine in early:
@@ -454,60 +493,16 @@
             copy.wait_send()
 
 
-GROUPS = 4
-
-
-def store_kernel(
-    store, times_ref, harm_ref, samples, state, store_out, ghosts_out, state_out, fresh, out_sem
-):
-    per = HARM // GROUPS
-    state_copy = pltpu.make_async_copy(state, state_out, out_sem.at[0])
-    state_copy.start()
-    writes = [state_copy]
-
-    def write(x, first, count):
-        rows = pl.ds(first, count)
-        copy = pltpu.make_async_copy(
-            fresh.at[x, rows], store_out.at[x, rows], out_sem.at[len(writes)]
-        )
+def finish_kernel(state, store, ghosts, state_out, store_out, ghosts_out, sems):
+    copies = [
+        pltpu.make_async_copy(store.at[0], store_out.at[0], sems.at[0]),
+        pltpu.make_async_copy(store.at[1], store_out.at[1], sems.at[1]),
+        pltpu.make_async_copy(state, state_out, sems.at[2]),
+        pltpu.make_async_copy(ghosts, ghosts_out, sems.at[3]),
+    ]
+    for copy in copies:
         copy.start()
-        writes.append(copy)
-
-    count8 = twice(harm_ref)
-    for x in range(2):
-        turn = turned(base_turn(twice(times_ref.at[x])), PERIOD)
-        lagged = turned(turn, LAG if x else -LAG)
-        seen = tuple(samples[x, 8 * j : 8 * j + 8, :] for j in range(5))
-        total = tuple(
-            0.875 * store[x, 0, 8 * j : 8 * j + 8, :] + 0.125 * seen[j] for j in range(5)
-        )
-        for j in range(5):
-            fresh[x, 0, 8 * j : 8 * j + 8, :] = total[j]
-        write(x, 0, 1)
-        carry = (turn, lagged, total)
-
-        def harmonic(k, carry):
-            now, late, total = carry
-            keep = k <= count8
-            c, s = jnp.where(keep, late[0], 0.0), jnp.where(keep, late[1], 0.0)
-            wc, ws = 0.25 * now[0], 0.25 * now[1]
-            sums = []
-            for j in range(5):
-                rows = slice(8 * j, 8 * j + 8)
-                new_c = 0.875 * store[x, k, rows, :] + wc * seen[j]
-                new_s = 0.875 * store[x, HARM + k, rows, :] + ws * seen[j]
-                fresh[x, k, rows, :] = new_c
-                fresh[x, HARM + k, rows, :] = new_s
-                sums.append(total[j] + (new_c * c + new_s * s))
-            return times_turn(now, turn), times_turn(late, lagged), tuple(sums)
-
-        for g in range(GROUPS):
-            carry = lax.fori_loop(1 + per * g, 1 + per * (g + 1), harmonic, carry, unroll=2)
-            for half in range(2):
-                write(x, 1 + HARM * half + per * g, per)
-        for j in range(5):
-            ghosts_out[x, 8 * j : 8 * j + 8, :] = carry[2][j]
-    for copy in writes:
+    for copy in copies:
         copy.wait()
 
 
@@ -516,14 +511,15 @@
     store_flat = fourier_store.reshape(2, COEFS, 40, 128)
     anywhere = pl.BlockSpec(memory_space=pl.ANY)
     vmem = pl.BlockSpec(memory_space=pltpu.VMEM)
-    state, samples = pl.pallas_call(
+    state, fresh, seen = pl.pallas_call(
         sections_kernel,
         out_shape=(
             jax.ShapeDtypeStruct(cells, F32),
+            jax.ShapeDtypeStruct(store_flat.shape, F32),
             jax.ShapeDtypeStruct((2, 40, 128), F32),
         ),
         in_specs=[pl.BlockSpec(memory_space=pltpu.HBM)] * 5,
-        out_specs=(vmem, vmem),
+        out_specs=(vmem, vmem, vmem),
         scratch_shapes=[
             pltpu.VMEM((5, 12, 32, 128), F32),
             pltpu.VMEM((5, 12, 32, 128), F32),
@@ -547,22 +543,18 @@
         ),
         name="sections",
     )(*[pltpu.with_memory_space_constraint(x, pltpu.HBM) for x in (flow_state, prior_state, store_flat, sample_times, harmonics)])
-    new_store, ghosts, new_state = pl.pallas_call(
-        store_kernel,
+    new_state, new_store, ghosts = pl.pallas_call(
+        finish_kernel,
         out_shape=(
+            jax.ShapeDtypeStruct(cells, F32),
             jax.ShapeDtypeStruct(store_flat.shape, F32),
             jax.ShapeDtypeStruct((2, 40, 128), F32),
-            jax.ShapeDtypeStruct(cells, F32),
         ),
-        in_specs=[vmem, vmem, vmem, vmem, anywhere],
-        out_specs=(anywhere, vmem, anywhere),
-        scratch_shapes=[
-            pltpu.VMEM((2, COEFS, 40, 128), F32),
-            pltpu.SemaphoreType.DMA((4 * GROUPS + 3,)),
-        ],
-        compiler_params=pltpu.CompilerParams(vmem_limit_bytes=24 * 1024 * 1024),
-        name="store",
-    )(store_flat, sample_times, harmonics, samples, state)
+        in_specs=[vmem] * 3,
+        out_specs=(anywhere,) * 3,
+        scratch_shapes=[pltpu.SemaphoreType.DMA((4,))],
+        name="finish",
+    )(*[pltpu.with_memory_space_constraint(x, pltpu.VMEM) for x in (state, fresh, seen)])
     return (
         new_state,
         new_store.reshape(fourier_store.shape),

time: 33.3 us -> 32.6 us (0.979)
  the two profiles are of different devices: /device:TPU:24 before, /device:TPU:80 now
where the time goes in v4:
time: 32.6 us; the launch traced here: 32.5 us
  Pallas kernels  31.8 us (98%)
  between operations  0.64 us (2%)
    pallas_call x1, Pallas kernels, shards(): pl.pallas_call(sections_kernel, out_shape=(jax.ShapeDtypeStruct(cells, F3...  30.4 us
    pallas_call x1, Pallas kernels, shards(): pl.pallas_call(finish_kernel, out_shape=(jax.ShapeDtypeStruct(cells, F32)...  1.43 us

profile of v4, /device:TPU:80, one launch (start us, length us, event | category | flops | bytes accessed | tf_op | source)
XLA Modules:
  0.0 32.5 jit_solution(13739532362480766960)
XLA Ops:
  0.6 30.4 %sections.1 = (f32[5,8,16,128]{3,2,1,0:T(8,128)S(1)}, f32[2,49,40,128]{3,2,1,0:T(8,128)S(1)}, f32[2,40,128]{2,1,0:T(8,128)S(1)}) custom-call(f32[5,8,16,128]{3,2,1,0:T(8,128)} %flow_hbm.1, f32[5,8,16,128]{3,2,1,0:T(8,128)} %prior_hbm.1, f32[2,49,40,128]{3,2,1,0:T(8,128)} %bitcast.3, s32[2,4,128]{2,1,0:T(4,128)} %times_hbm.1, s32[4,128]{1,0:T(4,128)} %harm_hbm.1), custom_call_target="tpu_custom_call" | custom-call | tf_op jit(solution)/shard_map/sections/pallas_call | solution.py:514
  31.0 1.4 %finish.1 = (f32[5,8,16,128]{3,2,1,0:T(8,128)}, f32[2,49,40,128]{3,2,1,0:T(8,128)}, f32[2,40,128]{2,1,0:T(8,128)}) custom-call(f32[5,8,16,128]{3,2,1,0:T(8,128)S(1)} %get-tuple-element.9.state, f32[2,49,40,128]{3,2,1,0:T(8,128)S(1)} %get-tuple-element.10.store, f32[2,40,128]{2,1,0:T(8,128)S(1)} %get-tuple-element.11.ghosts), custom_call_target="tpu_custom_call" | custom-call | tf_op jit(solution)/shard_map/finish/pallas_call | solution.py:546

commit v5 on v4

--- a/solution.py
+++ b/solution.py
@@ -371,8 +371,6 @@
 
                 if s < 2:
                     outer_sides(s + 1, t, False, (3 * side,))
-            if t == 0 and between:
-                between()
             if t == 0 and s > 0:
                 if s == 2:
                     arrive(*axial[s, 1], *axial[s, 2])
@@ -383,6 +381,8 @@
                     update(s, 2, 4, CENTER)
                 if s < 2:
                     send(*axial[s + 1, 1], *axial[s + 1, 2])
+                if between:
+                    between()
 
     loads[0].wait()
     loads[3].wait()

time: 32.6 us -> 32.7 us (level)
  the two profiles are of different devices: /device:TPU:80 before, /device:TPU:95 now
where the time goes in v5:
time: 32.7 us; the launch traced here: 32.5 us
  Pallas kernels  31.9 us (98%)
  between operations  0.64 us (2%)
    pallas_call x1, Pallas kernels, shards(): pl.pallas_call(sections_kernel, out_shape=(jax.ShapeDtypeStruct(cells, F3...  30.5 us
    pallas_call x1, Pallas kernels, shards(): pl.pallas_call(finish_kernel, out_shape=(jax.ShapeDtypeStruct(cells, F32)...  1.43 us

profile of v5, /device:TPU:95, one launch (start us, length us, event | category | flops | bytes accessed | tf_op | source)
XLA Modules:
  0.0 32.5 jit_solution(16183245920884334961)
XLA Ops:
  0.6 30.5 %sections.1 = (f32[5,8,16,128]{3,2,1,0:T(8,128)S(1)}, f32[2,49,40,128]{3,2,1,0:T(8,128)S(1)}, f32[2,40,128]{2,1,0:T(8,128)S(1)}) custom-call(f32[5,8,16,128]{3,2,1,0:T(8,128)} %flow_hbm.1, f32[5,8,16,128]{3,2,1,0:T(8,128)} %prior_hbm.1, f32[2,49,40,128]{3,2,1,0:T(8,128)} %bitcast.3, s32[2,4,128]{2,1,0:T(4,128)} %times_hbm.1, s32[4,128]{1,0:T(4,128)} %harm_hbm.1), custom_call_target="tpu_custom_call" | custom-call | tf_op jit(solution)/shard_map/sections/pallas_call | solution.py:514
  31.1 1.4 %finish.1 = (f32[5,8,16,128]{3,2,1,0:T(8,128)}, f32[2,49,40,128]{3,2,1,0:T(8,128)}, f32[2,40,128]{2,1,0:T(8,128)}) custom-call(f32[5,8,16,128]{3,2,1,0:T(8,128)S(1)} %get-tuple-element.9.state, f32[2,49,40,128]{3,2,1,0:T(8,128)S(1)} %get-tuple-element.10.store, f32[2,40,128]{2,1,0:T(8,128)S(1)} %get-tuple-element.11.ghosts), custom_call_target="tpu_custom_call" | custom-call | tf_op jit(solution)/shard_map/finish/pallas_call | solution.py:546
